TPU v7x, 256 devices: a whole 4x4x8 slice. The times are simulated.
256 devices in a mesh: dp: 32 (over y, z_hi, core), tensor: 8 (over x, z_lo).
Axes of the slice: x: 4, y: 4, z: 8 (z_hi: 4, z_lo: 2; z = z_hi * 2 + z_lo), core: 2. Of those that a mesh axis runs over, the one named last changes fastest.
Arguments:
- layer_input: bfloat16 [16384, 8192], P('dp', 'tensor'), may hold values from -6 to 6
- hidden_act: bfloat16 [16384, 28672], P('dp', 'tensor'), may hold values from -6 to 6
- grad_gate: bfloat16 [16384, 28672], P('dp', 'tensor'), may hold values from -6 to 6
- grad_up: bfloat16 [16384, 28672], P('dp', 'tensor'), may hold values from -6 to 6
- grad_output: bfloat16 [16384, 8192], P('dp', 'tensor'), may hold values from -6 to 6
- proj_gate_in: bfloat16 [8192, 64], P('tensor'), may hold values from -0.0625 to 0.0625
- proj_up_in: bfloat16 [8192, 64], P('tensor'), may hold values from -0.0625 to 0.0625
- proj_down_in: bfloat16 [28672, 64], P('tensor'), may hold values from -0.03125 to 0.03125
- proj_gate_out: bfloat16 [28672, 64], P('tensor'), may hold values from -0.03125 to 0.03125
- proj_up_out: bfloat16 [28672, 64], P('tensor'), may hold values from -0.03125 to 0.03125
- proj_down_out: bfloat16 [8192, 64], P('tensor'), may hold values from -0.0625 to 0.0625
- example_ids: int32 [32, 512], P('dp'), may hold values from 0 to 15, never falling along the last dimension, each value on 1 to 64 neighbouring positions
- query_sketches: bfloat16 [4096, 12288], P('dp', 'tensor'), may hold values from -0.019897461 to 0.019897461
Outputs:
- sketches: bfloat16 [512, 12288], P('dp', 'tensor')
- scores: float32 [512, 4096], P('dp', 'tensor')
Inputs may be any that keep to these rules, and one draw needn't show every extreme that they name: `example_ids`: in each row the ids never fall and every id from 0 to 15 occurs.
All inputs are finite; a program needn't handle non-finite values.
Results may differ from a plain program's by a relative error of at most 0.0058.
Values may be sent and summed in bfloat16 or wider, within the bound.
No kernel may reach another device: no remote copies, remote signals or barrier semaphores. Data moves between devices by JAX's collectives and lax.ppermute only.
A program may use at most 128 MiB of HBM per device.

v0:
```python
import jax
import jax.numpy as jnp
from jax import lax
from jax.sharding import PartitionSpec as P

EX_DEV = 16


def project(left, right):
    return jnp.dot(left, right, preferred_element_type=jnp.float32)


def outer_rows(y_cols, x_part, offset, row_count, rank):
    length = x_part.shape[0]
    x_sides = x_part.reshape(length, 3, rank)
    layer_of = (offset + jnp.arange(row_count, dtype=jnp.int32)) // rank
    chosen = jnp.take(x_sides, layer_of, axis=1)
    return (y_cols[:, :, None] * chosen).reshape(length, row_count * rank)


def one_hot_of(segment_ids):
    return (segment_ids[:, None] == jnp.arange(EX_DEV, dtype=jnp.int32)[None, :]).astype(
        jnp.float32
    )


def per_device(
    layer_input,
    hidden_act,
    grad_gate,
    grad_up,
    grad_output,
    proj_gate_in,
    proj_up_in,
    proj_down_in,
    proj_gate_out,
    proj_up_out,
    proj_down_out,
    example_ids,
    query_sketches,
):
    rank = proj_gate_in.shape[1]
    partial_value = jnp.concatenate(
        [
            project(grad_gate, proj_gate_out),
            project(grad_up, proj_up_out),
            project(grad_output, proj_down_out),
            project(layer_input, jnp.concatenate([proj_gate_in, proj_up_in], axis=1)),
            project(hidden_act, proj_down_in),
        ],
        axis=1,
    )
    segment_ids = example_ids[0]
    row_count = 3 * rank // lax.axis_size("tensor")
    offset = lax.axis_index("tensor") * row_count
    summed = lax.psum(partial_value, "tensor").astype(jnp.bfloat16).astype(jnp.float32)
    y_cols = lax.dynamic_slice_in_dim(summed, offset, row_count, 1)
    outer = outer_rows(y_cols, summed[:, 3 * rank :], offset, row_count, rank)
    sketch_sum = jnp.dot(one_hot_of(segment_ids).T, outer, precision=lax.Precision.HIGHEST)
    sketch = sketch_sum.astype(jnp.bfloat16)
    partial_scores = lax.dot_general(
        sketch,
        lax.all_gather(query_sketches, "dp", axis=0, tiled=True),
        (((1,), (1,)), ((), ())),
        preferred_element_type=jnp.float32,
    )
    scores = lax.psum_scatter(partial_scores, "tensor", scatter_dimension=1, tiled=True)
    return (sketch, scores)


def solution(mesh):
    placed = (
        P("dp", "tensor"),
        P("dp", "tensor"),
        P("dp", "tensor"),
        P("dp", "tensor"),
        P("dp", "tensor"),
        P("tensor", None),
        P("tensor", None),
        P("tensor", None),
        P("tensor", None),
        P("tensor", None),
        P("tensor", None),
        P("dp", None),
        P("dp", "tensor"),
    )
    return jax.shard_map(
        per_device,
        mesh=mesh,
        in_specs=placed,
        out_specs=(P("dp", "tensor"), P("dp", "tensor")),
        check_vma=False,
    )
```

profile of v0, /device:TPU:24, one launch (start us, length us, event | category | flops | bytes accessed | tf_op | source)
XLA Modules:
  0.0 178.9 jit_solution(6329116003237582668)
XLA Ops:
  7.2 0.0 copy-start
  7.2 0.0 copy-start.4
  7.2 0.0 all-gather.2.cloned.1.call-start
  7.2 0.7 all-gather.2.cloned.1.call-update
  7.9 0.0 reduce-scatter.2.cloned.1.call-start
  8.0 0.0 copy-start.1
  8.0 0.0 copy-start.7
  8.0 3.5 %convolution_dynamic-update-slice_fusion.3 = f32[512,384]{0,1:T(8,128)S(1)} fusion(bf16[512,3584]{1,0:T(8,128)(2,1)} %param.15, bf16[3584,64]{0,1:T(8,128)(2,1)} %param.21), kind=kOutput, calls=%fused_computation.9 | convolution fusion | flops 234881024 | bytes 4259840 | tf_op jit(solution)/shard_map/dot_general | solution.py:10
  11.5 0.0 copy-done.4
  11.5 0.0 copy-done.1
  11.5 0.0 copy-start.3
  11.5 0.0 copy-start.8
  11.5 0.0 copy-start.9
  11.5 0.0 copy-start.2
  11.6 0.0 copy-start.5
  11.6 1.2 convolution_dynamic-update-slice_fusion.2
  12.8 0.0 copy-done
  12.8 0.0 copy-done.7
  12.8 0.4 convolution_dynamic-update-slice_fusion
  13.2 0.0 copy-done.3
  13.2 0.0 copy-done.8
  13.3 0.0 copy-done.9
  13.3 0.5 fusion.1
  13.8 0.2 copy-done.2
  14.0 0.1 copy-done.5
  14.0 1.2 convolution_dynamic-update-slice_fusion.1
  15.2 93.4 %all-reduce.1 = bf16[512,384]{0,1:T(8,128)(2,1)S(1)} all-reduce(f32[512,384]{0,1:T(8,128)S(1)} %convolution_dynamic-update-slice_fusion.1), channel_id=1, replica_groups=mesh['dp'=32,'tensor'=8] {'tensor'}, use_global_device_ids=true, to_apply=%region_0.0 | all-reduce | flops 196608 | bytes 1179648 | tf_op jit(solution)/shard_map/psum | solution.py:56
  108.7 0.1 convert_element_type.16
  108.8 0.1 broadcast_in_dim.16
  108.9 0.1 broadcast_in_dim.17
  109.0 2.4 %gather_fusion = f32[24,512,64]{1,2,0:T(8,128)} fusion(f32[512,3,64]{0,2,1:T(8,128)S(1)} %bitcast.28, s32[1024]{0:T(1024)S(1)} %pad_clamp_fusion), kind=kCustom, calls=%fused_computation | custom fusion | bytes 6291552 | tf_op jit(solution)/shard_map/jit(_take)/gather | solution.py:17
  111.4 0.0 copy-start.10
  111.4 2.3 %fusion = f32[512,1536]{0,1:T(8,128)S(1)} fusion(f32[24,512,64]{1,2,0:T(8,128)} %gather_fusion, f32[512,24]{0,1:T(8,128)S(1)} %constant_dynamic-slice_fusion, pred[1536]{0:T(1024)(128)(4,1)S(1)} %broadcast_in_dim.17), kind=kLoop, calls=%fused_computation.2 | loop fusion | flops 1572864 | bytes 6342144 | tf_op jit(solution)/shard_map/mul | solution.py:18
  113.7 0.0 copy-done.10
  113.7 1.6 convolution_convert_fusion
  115.3 0.0 copy-start.6
  115.3 9.7 %all-gather.2.cloned.1.call-done = bf16[4096,1536]{1,0:T(8,128)(2,1)} async-done(((bf16[128,1536]{1,0:T(8,128)(2,1)}), bf16[4096,1536]{1,0:T(8,128)(2,1)}) %all-gather.2.cloned.1.call-update) | async-done | bytes 12582928 | tf_op jit(solution)/shard_map/all_gather | solution.py:63
  125.0 8.6 %fusion.10 = f32[16,4096]{1,0:T(8,128)} fusion(bf16[16,1536]{1,0:T(8,128)(2,1)S(1)} %convolution_convert_fusion, bf16[4096,1536]{1,0:T(8,128)(2,1)} %all-gather.2.cloned.1.call-done), kind=kOutput, calls=%fused_computation.32 | convolution fusion | flops 201326592 | bytes 12894208 | tf_op jit(solution)/shard_map/dot_general | solution.py:61
  133.7 0.0 copy-done.6
  133.7 0.0 reduce-scatter.2.cloned.1.call-update
  133.7 38.4 %reduce-scatter.2.cloned.1.call-done = f32[16,512]{1,0:T(8,128)} async-done(((f32[16,4096]{1,0:T(8,128)}), f32[16,512]{1,0:T(8,128)}) %reduce-scatter.2.cloned.1.call-update) | async-done | bytes 32784 | tf_op jit(solution)/shard_map/reduce_scatter | solution.py:67
  (5 shorter events, 0.1 us)
Async XLA Ops:
  7.2 5.6 %copy-start = (bf16[512,1024]{1,0:T(8,128)(2,1)S(1)}, bf16[512,1024]{1,0:T(8,128)(2,1)}, u32[]{:S(2)}) copy-start(bf16[512,1024]{1,0:T(8,128)(2,1)} %param.17) | copy-start | bytes 3145732
  7.2 4.3 %copy-start.4 = (bf16[3584,64]{0,1:T(8,128)(2,1)S(1)}, bf16[3584,64]{0,1:T(8,128)(2,1)}, u32[]{:S(2)}) copy-start(bf16[3584,64]{0,1:T(8,128)(2,1)} %param.22) | copy-start | bytes 1376260
  7.2 117.8 %all-gather.2.cloned.1.call-start = ((), (), s32[]{:S(2)}) async-start(), calls=%async_computation.1 | async-start | bytes 12976128 | tf_op jit(solution)/shard_map/all_gather | solution.py:63
  7.9 164.1 %reduce-scatter.2.cloned.1.call-start = ((), (), s32[]{:S(2)}) async-start(), calls=%async_computation.2 | async-start | bytes 294912 | tf_op jit(solution)/shard_map/reduce_scatter | solution.py:67
  8.0 3.5 %copy-start.1 = (bf16[512,3584]{1,0:T(8,128)(2,1)S(1)}, bf16[512,3584]{1,0:T(8,128)(2,1)}, u32[]{:S(2)}) copy-start(bf16[512,3584]{1,0:T(8,128)(2,1)} %param.16) | copy-start | bytes 11010052
  8.0 4.8 %copy-start.7 = (bf16[1024,64]{0,1:T(8,128)(2,1)S(1)}, bf16[1024,64]{0,1:T(8,128)(2,1)}, u32[]{:S(2)}) copy-start(bf16[1024,64]{0,1:T(8,128)(2,1)} %param.23) | copy-start | bytes 393220
  11.5 1.7 copy-start.3
  11.5 1.7 copy-start.8
  11.5 1.7 copy-start.9
  11.5 2.4 %copy-start.2 = (bf16[512,3584]{1,0:T(8,128)(2,1)S(1)}, bf16[512,3584]{1,0:T(8,128)(2,1)}, u32[]{:S(2)}) copy-start(bf16[512,3584]{1,0:T(8,128)(2,1)} %param.14) | copy-start | bytes 11010052
  11.6 2.5 %copy-start.5 = (bf16[3584,64]{0,1:T(8,128)(2,1)S(1)}, bf16[3584,64]{0,1:T(8,128)(2,1)}, u32[]{:S(2)}) copy-start(bf16[3584,64]{0,1:T(8,128)(2,1)} %param.20) | copy-start | bytes 1376260
  111.4 2.3 %copy-start.10 = (s32[1,512]{1,0:T(1,128)S(1)}, s32[1,512]{1,0:T(1,128)}, u32[]{:S(2)}) copy-start(s32[1,512]{1,0:T(1,128)} %param.24) | copy-start | bytes 6148
  115.3 18.3 %copy-start.6 = (bf16[16,1536]{1,0:T(8,128)(2,1)}, bf16[16,1536]{1,0:T(8,128)(2,1)S(1)}, u32[]{:S(2)}) copy-start(bf16[16,1536]{1,0:T(8,128)(2,1)S(1)} %convolution_convert_fusion) | copy-start | bytes 147460
Sparse Core Ops, SparseCore 0:
  10.6 114.4 all-gather.1
  133.8 38.2 reduce-scatter.1
where the time goes:
time: 179 us
  blocking collectives  93.4 us (52%)
  waiting for transfers between devices  48.8 us (27%)
  matrix products  17.1 us (10%)
  between operations  14.2 us (8%)
  local copies, waits for them, and re-layouts  2.91 us (2%)
  other arithmetic  2.41 us (1%)
    psum x1, blocking collectives, per_device(): lax.psum(partial_value, 'tensor').astype(jnp.bfloat16).astype(jnp.float32)  93.4 us
    reduce_scatter x1, waiting for transfers between devices, per_device(): lax.psum_scatter(partial_scores, 'tensor', scatter_dimension=1, tiled=True)  38.4 us
    all_gather x1, waiting for transfers between devices, per_device(): lax.all_gather(query_sketches, 'dp', axis=0, tiled=True)  9.68 us
    dot_general x1, matrix products, per_device(): lax.dot_general(sketch, lax.all_gather(query_sketches, 'dp', axis=0, tile...  8.64 us
    dot_general x5, matrix products, project(): return jnp.dot(left, right, preferred_element_type=jnp.float32)  6.83 us
  transfers between devices with their start and end apart: 2, of which 2 were waited for; matrix products, arithmetic and copies ran while one was open for 8% of the time, Pallas kernels for 0%

commit v1 on v0

v1 whole, which is shorter than its diff:
```python
import jax
import jax.numpy as jnp
from jax import lax
from jax.sharding import Mesh, PartitionSpec as P

EX_DEV = 16
RANK = 64
TENSOR = 8
ROWS = 3 * RANK // TENSOR
DP = ("y", "zhh", "zhl", "core")
S_AXES = ("zhl", "core")
G_AXES = ("y", "zhh")


def project_t(weight, act):
    dims = (((0,), (1,)), ((), ()))
    return lax.dot_general(weight, act, dims, preferred_element_type=jnp.float32)


def gather_sketch(sketch):
    out = sketch[None]
    for axis in reversed(S_AXES):
        other = lax.ppermute(out, axis, [(0, 1), (1, 0)])
        first = lax.axis_index(axis) == 0
        out = jnp.concatenate([jnp.where(first, out, other), jnp.where(first, other, out)], axis=0)
    return out


def per_device(
    layer_input,
    hidden_act,
    grad_gate,
    grad_up,
    grad_output,
    proj_gate_in,
    proj_up_in,
    proj_down_in,
    proj_gate_out,
    proj_up_out,
    proj_down_out,
    example_ids,
    query_sketches,
):
    tok = layer_input.shape[0]
    queries = lax.all_gather(query_sketches, G_AXES, axis=0, tiled=True)
    y_t = jnp.concatenate(
        [
            project_t(proj_gate_out, grad_gate),
            project_t(proj_up_out, grad_up),
            project_t(proj_down_out, grad_output),
        ],
        axis=0,
    ).astype(jnp.bfloat16)
    x_gu = project_t(jnp.concatenate([proj_gate_in, proj_up_in], axis=1), layer_input).astype(jnp.bfloat16)
    x_t = [x_gu[:RANK], x_gu[RANK:], project_t(proj_down_in, hidden_act).astype(jnp.bfloat16)]
    send = []
    for t in range(TENSOR):
        send.append(y_t[ROWS * t : ROWS * (t + 1)])
        send.append(x_t[ROWS * t // RANK])
        send.append(x_t[(ROWS * t + ROWS - 1) // RANK])
    send = jnp.concatenate(send, axis=0)
    got = lax.all_to_all(send, "tensor", 0, 0, tiled=True)
    width = ROWS + 2 * RANK
    summed = jnp.sum(got.reshape(TENSOR, width, tok).astype(jnp.float32), axis=0).astype(jnp.bfloat16)
    one_hot = example_ids == jnp.arange(EX_DEV, dtype=jnp.int32)[:, None]
    masked = jnp.where(one_hot[:, None, :], summed[None, :ROWS], jnp.bfloat16(0)).reshape(EX_DEV * ROWS, tok)
    both = lax.dot_general(
        masked, summed[ROWS:], (((1,), (1,)), ((), ())), preferred_element_type=jnp.float32
    ).reshape(EX_DEV, ROWS, 2 * RANK)
    first_row = lax.axis_index("tensor") * ROWS
    row = first_row + jnp.arange(ROWS, dtype=jnp.int32)
    in_first = (row // RANK == first_row // RANK)[None, :, None]
    sketch = jnp.where(in_first, both[:, :, :RANK], both[:, :, RANK:]).astype(jnp.bfloat16)
    sketch = sketch.reshape(EX_DEV, ROWS * RANK)

    group = gather_sketch(sketch)
    s = group.shape[0]
    partial = lax.dot_general(
        group.reshape(s * EX_DEV, ROWS * RANK),
        queries,
        (((1,), (1,)), ((), ())),
        preferred_element_type=jnp.float32,
    )
    nq = partial.shape[1] // TENSOR
    partial = partial.reshape(s, EX_DEV, TENSOR, nq).transpose(0, 2, 1, 3).reshape(s * TENSOR * EX_DEV, nq)
    back = lax.all_to_all(partial, S_AXES + ("tensor",), 0, 0, tiled=True)
    back = jnp.sum(back.reshape(s, TENSOR, EX_DEV, nq), axis=1)
    if S_AXES == ("zhl", "core"):
        scores = back.transpose(1, 0, 2)
    elif S_AXES == ("core",):
        scores = back.reshape(2, EX_DEV, 2, 128).transpose(1, 2, 0, 3)
    else:
        scores = back.transpose(1, 0, 2)
    return (sketch, scores.reshape(EX_DEV, s * nq))


def solution(mesh):
    split = Mesh(mesh.devices.reshape(4, 2, 2, 2, TENSOR), DP + ("tensor",))
    placed = (P(DP, "tensor"),) * 5 + (P("tensor", None),) * 6 + (P(DP, None), P(DP, "tensor"))
    return jax.shard_map(
        per_device,
        mesh=split,
        in_specs=placed,
        out_specs=(P(DP, "tensor"), P(DP, "tensor")),
        check_vma=False,
    )
```

time: 179 us -> 136 us (0.76); the launches traced: 179 us -> 134 us
  blocking collectives: 93.4 us -> 0 us
  waiting for transfers between devices: 48.8 us -> 77.9 us
  starting transfers between devices: 0.08 us -> 14.6 us
  local copies, waits for them, and re-layouts: 2.91 us -> 14 us
  matrix products: 17.1 us -> 11.5 us
    psum x1 -> x0, blocking collectives: 93.4 us -> none  [per_device(): lax.psum(partial_value, 'tensor').astype(jnp.bfloat16).astype(jnp.float32)]
    ppermute x0 -> x2, waiting for transfers between devices: none -> 39.9 us  [gather_sketch(): other = lax.ppermute(out, axis, [(0, 1), (1, 0)])]
    reduce_scatter x1 -> x0, waiting for transfers between devices: 38.4 us -> none  [per_device(): lax.psum_scatter(partial_scores, 'tensor', scatter_dimension=1, tiled=True)]
    all_to_all x0 -> x2, waiting for transfers between devices: none -> 28.3 us  [the longest x1 17.9 us: per_device(): got = lax.all_to_all(send, 'tensor', 0, 0, tiled=True)]
    unnamed x22 -> x39, local copies, waits for them, and re-layouts: 0.32 us -> 11.9 us
    all_to_all x0 -> x2, starting transfers between devices: none -> 10.7 us  [the longest x1 5.79 us: per_device(): got = lax.all_to_all(send, 'tensor', 0, 0, tiled=True)]
    dot_general x7, matrix products: 17.1 us -> 11.5 us  [the longest x5 7.52 us: project_t(): lax.dot_general(weight, act, dims, preferred_element_type=jnp.float32)]
    ppermute x0 -> x2, starting transfers between devices: none -> 3.88 us  [gather_sketch(): other = lax.ppermute(out, axis, [(0, 1), (1, 0)])]
  transfers between devices with their start and end apart: 2 -> 5, of which waited for: 2 -> 5; matrix products, arithmetic and copies ran while one was open for 8% -> 17% of each run, Pallas kernels for 0% -> 0%
where the time goes in v1:
time: 136 us; the launch traced here: 134 us
  waiting for transfers between devices  77.9 us (57%)
  starting transfers between devices  14.6 us (11%)
  between operations  14.2 us (10%)
  local copies, waits for them, and re-layouts  14 us (10%)
  matrix products  11.5 us (8%)
  other arithmetic  1.56 us (1%)
    ppermute x2, waiting for transfers between devices, gather_sketch(): other = lax.ppermute(out, axis, [(0, 1), (1, 0)])  39.9 us
    all_to_all x1, waiting for transfers between devices, per_device(): got = lax.all_to_all(send, 'tensor', 0, 0, tiled=True)  17.9 us
    unnamed x39, local copies, waits for them, and re-layouts  11.9 us
    all_to_all x1, waiting for transfers between devices, per_device(): back = lax.all_to_all(partial, S_AXES + ('tensor',), 0, 0, tiled=True)  10.4 us
    all_gather x1, waiting for transfers between devices, per_device(): queries = lax.all_gather(query_sketches, G_AXES, axis=0, tiled=True)  9.12 us
    dot_general x5, matrix products, project_t(): lax.dot_general(weight, act, dims, preferred_element_type=jnp.float32)  7.52 us
    all_to_all x1, starting transfers between devices, per_device(): got = lax.all_to_all(send, 'tensor', 0, 0, tiled=True)  5.79 us
    all_to_all x1, starting transfers between devices, per_device(): back = lax.all_to_all(partial, S_AXES + ('tensor',), 0, 0, tiled=True)  4.93 us
  transfers between devices with their start and end apart: 5, of which 5 were waited for; matrix products, arithmetic and copies ran while one was open for 17% of the time, Pallas kernels for 0%

profile of v1, /device:TPU:24, one launch (start us, length us, event | category | flops | bytes accessed | tf_op | source)
XLA Modules:
  0.0 133.8 jit_solution(6854948010987335564)
XLA Ops:
  7.2 0.0 copy-start
  7.2 0.0 all-gather.2.cloned.1.call-start
  7.2 0.7 all-gather.2.cloned.1.call-update
  7.9 3.5 %convolution_convert_fusion.4 = bf16[64,512]{1,0:T(8,128)(2,1)S(1)} fusion(bf16[3584,64]{0,1:T(8,128)(2,1)} %param.21, bf16[512,3584]{1,0:T(8,128)(2,1)} %param.15), kind=kOutput, calls=%fused_computation.4 | convolution fusion | flops 234913792 | bytes 4194304 | tf_op jit(solution)/shard_map/dot_general | solution.py:17
  11.5 0.0 copy-start.5
  11.5 0.6 constant_dynamic-update-slice_fusion.22
  12.1 0.5 convolution_convert_fusion
  12.6 0.6 constant_dynamic-update-slice_fusion.21
  13.2 0.6 constant_dynamic-update-slice_fusion.20
  13.9 0.6 constant_dynamic-update-slice_fusion.19
  14.5 0.6 constant_dynamic-update-slice_fusion.18
  15.1 0.6 constant_dynamic-update-slice_fusion.17
  15.7 0.0 copy-start.2
  15.7 1.2 convolution_convert_fusion.3
  17.0 0.6 constant_dynamic-update-slice_fusion.16
  17.6 0.7 constant_dynamic-update-slice_fusion.15
  18.2 0.6 constant_dynamic-update-slice_fusion.14
  18.8 0.6 constant_dynamic-update-slice_fusion.13
  19.5 0.6 constant_dynamic-update-slice_fusion.12
  20.1 0.6 constant_dynamic-update-slice_fusion.11
  20.7 0.6 constant_dynamic-update-slice_fusion.10
  21.3 0.4 convolution_convert_fusion.1
  21.8 0.6 constant_dynamic-update-slice_fusion.9
  22.4 0.6 constant_dynamic-update-slice_fusion.8
  23.0 0.6 constant_dynamic-update-slice_fusion.7
  23.6 1.8 %constant_dynamic-update-slice_fusion.6 = (bf16[1216,512]{1,0:T(8,128)(2,1)}, bf16[64,512]{1,0:T(8,128)(2,1)S(1)}) fusion(bf16[1216,512]{1,0:T(8,128)(2,1)} %constant_dynamic-update-slice_fusion.7, bf16[3584,64]{0,1:T(8,128)(2,1)S(1)} %copy-done.4, bf16[512,3584]{1,0:T(8,128)(2,1)S(1)} %copy-done.2), kind=kOutput, calls=%fused_computation.32 | convolution fusion | flops 234913792 | bytes 4259840 | tf_op jit(solution)/shard_map/dot_general | solution.py:17
  25.5 0.6 constant_dynamic-update-slice_fusion.5
  26.1 0.6 constant_dynamic-update-slice_fusion.4
  26.7 0.6 constant_dynamic-update-slice_fusion.3
  27.3 0.6 constant_dynamic-update-slice_fusion.2
  28.0 0.6 constant_dynamic-update-slice_fusion.1
  28.6 0.6 constant_dynamic-update-slice_fusion
  29.2 5.8 %all-to-all-start = ((bf16[8,152,512]{2,1,0:T(8,128)(2,1)}), bf16[8,152,512]{2,1,0:T(8,128)(2,1)S(1)}, u32[]{:S(2)}, u32[]{:S(2)}) async-start(bf16[8,152,512]{2,1,0:T(8,128)(2,1)} %bitcast.1), calls=%async_computation | async-start | bytes 2490368 | tf_op jit(solution)/shard_map/all_to_all | solution.py:62
  35.0 17.9 %all-to-all-done = bf16[8,152,512]{2,1,0:T(8,128)(2,1)S(1)} async-done(((bf16[8,152,512]{2,1,0:T(8,128)(2,1)}), bf16[8,152,512]{2,1,0:T(8,128)(2,1)S(1)}, u32[]{:S(2)}, u32[]{:S(2)}) %all-to-all-start) | async-done | bytes 1245216 | tf_op jit(solution)/shard_map/all_to_all | solution.py:62
  52.9 0.2 reduce_sum.21
  53.1 0.3 fusion
  53.4 0.1 fusion.6
  53.5 0.1 broadcast_in_dim_reshape.3
  53.6 0.1 collective-permute-start
  53.7 1.2 collective-permute-done
  55.0 3.8 %collective-permute-start.1 = (bf16[2,16,1536]{2,1,0:T(8,128)(2,1)S(1)}, bf16[2,16,1536]{2,1,0:T(8,128)(2,1)S(1)}, u32[]{:S(2)}, u32[]{:S(2)}) collective-permute-start(bf16[2,16,1536]{2,1,0:T(8,128)(2,1)S(1)} %pad_maximum_fusion), channel_id=1, source_target_pairs={{0,16},{16,0},{1,17},{17,1},{2,18},{18,2},{3,19},{19,3},{4,20},{20... | collective-permute-start | bytes 294920 | tf_op jit(solution)/shard_map/ppermute | solution.py:23
  58.8 38.7 %collective-permute-done.1 = bf16[2,16,1536]{2,1,0:T(8,128)(2,1)S(1)} collective-permute-done((bf16[2,16,1536]{2,1,0:T(8,128)(2,1)S(1)}, bf16[2,16,1536]{2,1,0:T(8,128)(2,1)S(1)}, u32[]{:S(2)}, u32[]{:S(2)}) %collective-permute-start.1) | collective-permute-done | bytes 98336 | tf_op jit(solution)/shard_map/ppermute | solution.py:23
  97.5 9.1 %all-gather.2.cloned.1.call-done = bf16[1024,1536]{1,0:T(8,128)(2,1)} async-done(((bf16[128,1536]{1,0:T(8,128)(2,1)}), bf16[1024,1536]{1,0:T(8,128)(2,1)}) %all-gather.2.cloned.1.call-update) | async-done | bytes 3145744 | tf_op jit(solution)/shard_map/all_gather | solution.py:45
  106.6 3.7 %fusion.7 = f32[4,16,8,128]{3,1,2,0:T(8,128)} fusion(bf16[8,128,1536,1]{2,1,0,3:T(8,128)(2,1)} %bitcast.34, bf16[2,16,1536]{2,1,0:T(8,128)(2,1)S(1)} %get-tuple-element.3, bf16[2,16,1536]{2,1,0:T(8,128)(2,1)S(1)} %get-tuple-element.2), kind=kOutput, calls=%fused_computation.15 | convolution fusion | flops 201719808 | bytes 3604480 | tf_op jit(solution)/shard_map/dot_general | solution.py:78
  110.3 4.9 %all-to-all-start.1 = ((f32[32,16,128]{2,1,0:T(8,128)}), f32[32,16,128]{2,1,0:T(8,128)S(1)}, u32[]{:S(2)}, u32[]{:S(2)}) async-start(f32[32,16,128]{2,1,0:T(8,128)} %bitcast.8), calls=%async_computation.1 | async-start | bytes 524288 | tf_op jit(solution)/shard_map/all_to_all | solution.py:86
  115.2 0.8 reshape.71
  115.9 10.4 %all-to-all-done.1 = f32[32,16,128]{2,1,0:T(8,128)S(1)} async-done(((f32[32,16,128]{2,1,0:T(8,128)}), f32[32,16,128]{2,1,0:T(8,128)S(1)}, u32[]{:S(2)}, u32[]{:S(2)}) %all-to-all-start.1) | async-done | bytes 262176 | tf_op jit(solution)/shard_map/all_to_all | solution.py:86
  126.3 0.6 copy_bitcast_fusion
  (24 shorter events, 0.1 us)
Async XLA Ops:
  7.2 4.9 %copy-start = (bf16[512,1024]{1,0:T(8,128)(2,1)S(1)}, bf16[512,1024]{1,0:T(8,128)(2,1)}, u32[]{:S(2)}) copy-start(bf16[512,1024]{1,0:T(8,128)(2,1)} %param.13) | copy-start | bytes 3145732
  7.2 99.4 %all-gather.2.cloned.1.call-start = ((), (), s32[]{:S(2)}) async-start(), calls=%async_computation.2 | async-start | bytes 3538944 | tf_op jit(solution)/shard_map/all_gather | solution.py:45
  7.9 4.2 %copy-start.7 = (bf16[1024,64]{0,1:T(8,128)(2,1)S(1)}, bf16[1024,64]{0,1:T(8,128)(2,1)}, u32[]{:S(2)}) copy-start(bf16[1024,64]{0,1:T(8,128)(2,1)} %param.19) | copy-start | bytes 393220
  7.9 4.2 %copy-start.8 = (bf16[1024,64]{0,1:T(8,128)(2,1)S(1)}, bf16[1024,64]{0,1:T(8,128)(2,1)}, u32[]{:S(2)}) copy-start(bf16[1024,64]{0,1:T(8,128)(2,1)} %param.18) | copy-start | bytes 393220
  7.9 7.8 %copy-start.1 = (bf16[512,3584]{1,0:T(8,128)(2,1)S(1)}, bf16[512,3584]{1,0:T(8,128)(2,1)}, u32[]{:S(2)}) copy-start(bf16[512,3584]{1,0:T(8,128)(2,1)} %param.16) | copy-start | bytes 11010052
  11.5 4.2 %copy-start.5 = (bf16[3584,64]{0,1:T(8,128)(2,1)S(1)}, bf16[3584,64]{0,1:T(8,128)(2,1)}, u32[]{:S(2)}) copy-start(bf16[3584,64]{0,1:T(8,128)(2,1)} %param.22) | copy-start | bytes 1376260
  15.7 5.6 %copy-start.3 = (bf16[512,1024]{1,0:T(8,128)(2,1)S(1)}, bf16[512,1024]{1,0:T(8,128)(2,1)}, u32[]{:S(2)}) copy-start(bf16[512,1024]{1,0:T(8,128)(2,1)} %param.17) | copy-start | bytes 3145732
  15.7 5.6 %copy-start.6 = (bf16[1024,64]{0,1:T(8,128)(2,1)S(1)}, bf16[1024,64]{0,1:T(8,128)(2,1)}, u32[]{:S(2)}) copy-start(bf16[1024,64]{0,1:T(8,128)(2,1)} %param.23) | copy-start | bytes 393220
  15.7 7.9 %copy-start.2 = (bf16[512,3584]{1,0:T(8,128)(2,1)S(1)}, bf16[512,3584]{1,0:T(8,128)(2,1)}, u32[]{:S(2)}) copy-start(bf16[512,3584]{1,0:T(8,128)(2,1)} %param.14) | copy-start | bytes 11010052
  17.6 6.1 %copy-start.4 = (bf16[3584,64]{0,1:T(8,128)(2,1)S(1)}, bf16[3584,64]{0,1:T(8,128)(2,1)}, u32[]{:S(2)}) copy-start(bf16[3584,64]{0,1:T(8,128)(2,1)} %param.20) | copy-start | bytes 1376260
  29.2 5.8 %copy-start.9 = (s32[1,512]{1,0:T(1,128)S(1)}, s32[1,512]{1,0:T(1,128)}, u32[]{:S(2)}) copy-start(s32[1,512]{1,0:T(1,128)} %param.24) | copy-start | bytes 6148
  29.2 23.7 %all-to-all-start = ((bf16[8,152,512]{2,1,0:T(8,128)(2,1)}), bf16[8,152,512]{2,1,0:T(8,128)(2,1)S(1)}, u32[]{:S(2)}, u32[]{:S(2)}) async-start(bf16[8,152,512]{2,1,0:T(8,128)(2,1)} %bitcast.1), calls=%async_computation | async-start | bytes 2490368 | tf_op jit(solution)/shard_map/all_to_all | solution.py:62
  53.6 1.3 collective-permute-start
  55.0 42.5 %collective-permute-start.1 = (bf16[2,16,1536]{2,1,0:T(8,128)(2,1)S(1)}, bf16[2,16,1536]{2,1,0:T(8,128)(2,1)S(1)}, u32[]{:S(2)}, u32[]{:S(2)}) collective-permute-start(bf16[2,16,1536]{2,1,0:T(8,128)(2,1)S(1)} %pad_maximum_fusion), channel_id=1, source_target_pairs={{0,16},{16,0},{1,17},{17,1},{2,18},{18,2},{3,19},{19,3},{4,20},{20... | collective-permute-start | bytes 294920 | tf_op jit(solution)/shard_map/ppermute | solution.py:23
  110.3 16.1 %all-to-all-start.1 = ((f32[32,16,128]{2,1,0:T(8,128)}), f32[32,16,128]{2,1,0:T(8,128)S(1)}, u32[]{:S(2)}, u32[]{:S(2)}) async-start(f32[32,16,128]{2,1,0:T(8,128)} %bitcast.8), calls=%async_computation.1 | async-start | bytes 524288 | tf_op jit(solution)/shard_map/all_to_all | solution.py:86
Sparse Core Ops, SparseCore 0:
  10.6 95.9 all-gather.1

commit v2 on v1

v2 whole, which is shorter than its diff:
```python
import functools

import jax
import jax.numpy as jnp
from jax import lax
from jax.experimental import pallas as pl
from jax.experimental.pallas import tpu as pltpu
from jax.sharding import Mesh, PartitionSpec as P

EX_DEV = 16
RANK = 64
TENSOR = 8
ROWS = 24
EXTRA = 8
SLOTS = ROWS + EXTRA
PIECE = SLOTS + RANK
DP = ("y", "zhh", "zhl", "core")
S_AXES = ("zhh", "zhl")
Q_FAR = "relay"
VMEM = 60 << 20

Y_RUNS = (
    ((0, 24), None),
    ((24, 48), None),
    ((48, 64), None, None),
    ((72, 96), (64, 72)),
    ((96, 120), (120, 128)),
    (None, (128, 144), None),
    ((144, 168), None),
    ((168, 192), None),
)
X_OF = (0, 0, 0, 1, 1, 2, 2, 2)


def project_kernel(gg, gu, go, li, ha, wgg, wgu, wgo, wgi, wui, wha, out):
    def dot(a, w):
        return lax.dot_general(a[...], w[...], (((1,), (1,)), ((), ())), preferred_element_type=jnp.float32)

    gate_up = jnp.concatenate([dot(gg, wgg), dot(gu, wgu)], axis=1).T
    down = jnp.concatenate([dot(go, wgo), dot(ha, wha)], axis=1).T
    x_gate_up = jnp.concatenate([dot(li, wgi), dot(li, wui)], axis=1).T.astype(jnp.bfloat16)
    y_t = jnp.concatenate([gate_up, down[:RANK]], axis=0)
    x_t = (x_gate_up[:RANK], x_gate_up[RANK:], down[RANK:].astype(jnp.bfloat16))
    zeros = jnp.zeros((EXTRA, y_t.shape[1]), jnp.float32)
    for t in range(TENSOR):
        runs = [zeros if run is None else y_t[run[0] : run[1]] for run in Y_RUNS[t]]
        out[t, :SLOTS, :] = jnp.concatenate(runs, axis=0).astype(jnp.bfloat16)
        out[t, SLOTS:, :] = x_t[X_OF[t]]


def project(acts, weights):
    tok = acts[0].shape[0]
    step = 128

    def rows(a):
        return pl.BlockSpec((step, a.shape[1]), lambda i: (i, 0))

    def whole(a):
        return pl.BlockSpec(a.shape, lambda i: (0, 0))

    return pl.pallas_call(
        project_kernel,
        grid=(tok // step,),
        in_specs=[rows(a) for a in acts] + [whole(w) for w in weights],
        out_specs=pl.BlockSpec((TENSOR, PIECE, step), lambda i: (0, 0, i)),
        out_shape=jax.ShapeDtypeStruct((TENSOR, PIECE, tok), jnp.bfloat16),
        compiler_params=pltpu.CompilerParams(vmem_limit_bytes=VMEM),
        cost_estimate=pl.CostEstimate(flops=10**9, bytes_accessed=15 << 20, transcendentals=0),
    )(*acts, *weights)


def sketch_kernel(got, ids, out):
    total = got[0].astype(jnp.float32)
    for t in range(1, TENSOR):
        total = total + got[t].astype(jnp.float32)
    tok = total.shape[1]
    x = total[SLOTS:].astype(jnp.bfloat16)
    y = total[:SLOTS].astype(jnp.bfloat16).astype(jnp.float32)
    mask = ids[...] == lax.broadcasted_iota(jnp.int32, (EX_DEV, tok), 0)
    rows = [jnp.where(mask, y[a : a + 1], 0.0).astype(jnp.bfloat16) for a in range(SLOTS)]
    outer = lax.dot_general(
        jnp.concatenate(rows, axis=0), x, (((1,), (1,)), ((), ())), preferred_element_type=jnp.float32
    ).reshape(SLOTS, EX_DEV, RANK)
    for a in range(0, SLOTS, 2):
        pair = jnp.concatenate([outer[a], outer[a + 1]], axis=1)
        out[:, a * RANK : (a + 2) * RANK] = pair.astype(jnp.bfloat16)


def sketch_of(got, ids):
    return pl.pallas_call(
        sketch_kernel,
        out_shape=jax.ShapeDtypeStruct((EX_DEV, SLOTS * RANK), jnp.bfloat16),
        compiler_params=pltpu.CompilerParams(vmem_limit_bytes=32 << 20),
    )(got, ids)


def ring(axis, shift):
    n = lax.axis_size(axis)
    return [(i, (i + shift) % n) for i in range(n)]


def around(x, axis, relay):
    before = lax.ppermute(x, axis, ring(axis, 1))
    after = lax.ppermute(x, axis, ring(axis, -1))
    half = x.shape[1] // 2
    if relay:
        far = (
            lax.ppermute(before[:, :half], axis, ring(axis, 1)),
            lax.ppermute(after[:, half:], axis, ring(axis, -1)),
        )
    else:
        both = lax.ppermute(x, axis, ring(axis, 2))
        far = (both[:, :half], both[:, half:])
    return x, after, far, before


def score_kernel(s0, s1, s2a, s2b, s3, *refs):
    pieces, out = refs[:-1], refs[-1]
    y, core = lax.axis_index("y"), lax.axis_index("core")
    zhh = lax.axis_index("zhh")
    zh = zhh * 2 + lax.axis_index("zhl")
    far = jnp.concatenate([s2a[...], s2b[...]], axis=1)
    group = jnp.concatenate([s0[...], s1[...], far, s3[...]], axis=0)
    out[...] = jnp.zeros(out.shape, out.dtype)
    half = group.shape[1] // 2
    dims = (((1,), (1,)), ((), ()))

    def dot(left, right):
        return lax.dot_general(left, right, dims, preferred_element_type=jnp.float32)

    for c in range(2):
        q0, q1, q2a, q2b, q3 = pieces[5 * c : 5 * c + 5]
        lane = pl.multiple_of(lax.rem(core + c, 2) * 128, 128)
        for r, q in enumerate((q0, q1, (q2a, q2b), q3)):
            if r == 2:
                part = dot(group[:, :half], q2a[...]) + dot(group[:, half:], q2b[...])
            else:
                part = dot(group, q[...])
            part = part.astype(jnp.bfloat16)
            slot = lax.rem(y + r, 4) * 2 + zhh
            for z in range(4):
                out[lax.rem(zh + z, 4), slot, :, pl.ds(lane, 128)] = part[z * EX_DEV : (z + 1) * EX_DEV]


def finish_kernel(back, out):
    zlo = lax.rem(lax.axis_index("tensor"), 2)
    for zhl in range(2):
        total = back[zlo * 2 + zhl, 0].astype(jnp.float32)
        for t in range(1, TENSOR):
            total = total + back[zlo * 2 + zhl, t].astype(jnp.float32)
        out[:, zhl * 256 : (zhl + 1) * 256] = total


def flat(group):
    own, after, far, before = group
    return (own, after) + tuple(far) + (before,)


def per_device(
    layer_input,
    hidden_act,
    grad_gate,
    grad_up,
    grad_output,
    proj_gate_in,
    proj_up_in,
    proj_down_in,
    proj_gate_out,
    proj_up_out,
    proj_down_out,
    example_ids,
    query_sketches,
):
    t = lax.axis_index("tensor")
    acts = (grad_gate, grad_up, grad_output, layer_input, hidden_act)
    weights = (proj_gate_out, proj_up_out, proj_down_out, proj_gate_in, proj_up_in, proj_down_in)
    queries = flat(around(query_sketches, "y", Q_FAR == "relay"))
    others = tuple(lax.ppermute(q, "core", ring("core", 1)) for q in queries)
    send = project(acts, tuple(w.T for w in weights))
    got = lax.all_to_all(send, "tensor", 0, 0, tiled=True)
    wide = sketch_of(got, example_ids)
    main, extra = wide[:, : ROWS * RANK], wide[:, ROWS * RANK :]
    moved = lax.ppermute(extra, "tensor", [(3, 2), (4, 5)])
    none = jnp.zeros_like(moved)
    place = jnp.concatenate([jnp.where(t == 5, moved, none), none, jnp.where(t == 2, moved, none)], axis=1)
    sketch = main + place

    group = flat(around(sketch, S_AXES, False))
    partial = pl.pallas_call(
        score_kernel,
        out_shape=jax.ShapeDtypeStruct((4, TENSOR, EX_DEV, 256), jnp.bfloat16),
        compiler_params=pltpu.CompilerParams(vmem_limit_bytes=32 << 20),
    )(*group, *queries, *others)
    back = lax.all_to_all(partial.reshape(4 * TENSOR, EX_DEV, 256), S_AXES + ("tensor",), 0, 0, tiled=True)
    scores = pl.pallas_call(
        finish_kernel,
        out_shape=jax.ShapeDtypeStruct((EX_DEV, 512), jnp.float32),
        compiler_params=pltpu.CompilerParams(vmem_limit_bytes=32 << 20),
    )(back.reshape(4, TENSOR, EX_DEV, 256))
    return (sketch, scores)


def solution(mesh):
    split = Mesh(mesh.devices.reshape(4, 2, 2, 2, TENSOR), DP + ("tensor",))
    placed = (P(DP, "tensor"),) * 5 + (P("tensor", None),) * 6 + (P(DP, None), P(DP, "tensor"))
    return jax.shard_map(
        per_device,
        mesh=split,
        in_specs=placed,
        out_specs=(P(DP, "tensor"), P(DP, "tensor")),
        check_vma=False,
    )
```

time: 136 us -> 74.4 us (0.55)
  waiting for transfers between devices: 77.9 us -> 16.1 us
  blocking collectives: 0 us -> 21.2 us
  local copies, waits for them, and re-layouts: 14 us -> 0.06 us
  between operations: 14.2 us -> 0.75 us
  Pallas kernels: 0 us -> 11.6 us
  matrix products: 11.5 us -> 0 us
  starting transfers between devices: 14.6 us -> 23.3 us
  other arithmetic: 1.56 us -> 0.03 us
    ppermute x2 -> x13, waiting for transfers between devices: 39.9 us -> 15.5 us  [the longest x2 12 us: around(): before = lax.ppermute(x, axis, ring(axis, 1))]
    all_to_all x0 -> x1, blocking collectives: none -> 21.2 us  [per_device(): lax.all_to_all(partial.reshape(4 * TENSOR, EX_DEV, 256), S_AXES + ('tenso...]
    all_to_all x1, waiting for transfers between devices: 17.9 us -> 0.64 us  [per_device(): got = lax.all_to_all(send, 'tensor', 0, 0, tiled=True)]
    ppermute x2 -> x13, starting transfers between devices: 3.88 us -> 17.7 us  [the longest x2 6.54 us: around(): after = lax.ppermute(x, axis, ring(axis, -1))]
    unnamed x39 -> x6, local copies, waits for them, and re-layouts: 11.9 us -> 0.02 us
    pallas_call x0 -> x4, Pallas kernels: none -> 11.6 us  [the longest x1 9.32 us: project(): pl.pallas_call(project_kernel, grid=(tok // step,), in_specs=[rows(a) for...]
    dot_general x7 -> x0, matrix products: 11.5 us -> none  [the longest x5 7.52 us: project_t(): lax.dot_general(weight, act, dims, preferred_element_type=jnp.float32)]
    all_to_all x1 -> x0, waiting for transfers between devices: 10.4 us -> none  [per_device(): back = lax.all_to_all(partial, S_AXES + ('tensor',), 0, 0, tiled=True)]
  transfers between devices with their start and end apart: 5 -> 14, of which waited for: 5 -> 5; matrix products, arithmetic and copies ran while one was open for 17% -> 0% of each run, Pallas kernels for 0% -> 1%
where the time goes in v2:
time: 74.4 us; the launch traced here: 73 us
  starting transfers between devices  23.3 us (31%)
  blocking collectives  21.2 us (28%)
  waiting for transfers between devices  16.1 us (22%)
  Pallas kernels  11.6 us (16%)
  between operations  0.75 us (1%)
    all_to_all x1, blocking collectives, per_device(): lax.all_to_all(partial.reshape(4 * TENSOR, EX_DEV, 256), S_AXES + ('tenso...  21.2 us
    ppermute x2, waiting for transfers between devices, around(): before = lax.ppermute(x, axis, ring(axis, 1))  12 us
    pallas_call x1, Pallas kernels, project(): pl.pallas_call(project_kernel, grid=(tok // step,), in_specs=[rows(a) for...  9.32 us
    ppermute x2, starting transfers between devices, around(): after = lax.ppermute(x, axis, ring(axis, -1))  6.54 us
    ppermute x1, starting transfers between devices, around(): both = lax.ppermute(x, axis, ring(axis, 2))  6.38 us
    all_to_all x1, starting transfers between devices, per_device(): got = lax.all_to_all(send, 'tensor', 0, 0, tiled=True)  5.67 us
    ppermute x2, waiting for transfers between devices, around(): after = lax.ppermute(x, axis, ring(axis, -1))  2.14 us
    ppermute x1, starting transfers between devices, around(): lax.ppermute(before[:, :half], axis, ring(axis, 1))  1.57 us
  transfers between devices with their start and end apart: 14, of which 5 were waited for; matrix products, arithmetic and copies ran while one was open for 0% of the time, Pallas kernels for 1%

profile of v2, /device:TPU:24, one launch (start us, length us, event | category | flops | bytes accessed | tf_op | source)
XLA Modules:
  0.0 73.0 jit_solution(4135561670979833367)
XLA Ops:
  0.6 0.0 copy-start
  0.6 0.0 copy-start.2
  0.7 9.3 %shard_map.140 = bf16[8,96,512]{2,1,0:T(8,128)(2,1)} custom-call(bf16[512,3584]{1,0:T(8,128)(2,1)} %gg.1, bf16[512,3584]{1,0:T(8,128)(2,1)} %gu.1, bf16[512,1024]{1,0:T(8,128)(2,1)} %go.1, bf16[512,1024]{1,0:T(8,128)(2,1)} %li.1, bf16[512,3584]{1,0:T(8,128)(2,1)} %ha.1, bf16[64,3584]{1,0:T(8,128)(2,1)} %bitcast.10, bf16[64,3584]{1,0:T(8,128)(2,1)} %bitcast.11, ...), custom_call_target="tpu_custom_call" | custom-call | flops 1000000000 | bytes 15728640 | tf_op jit(solution)/shard_map/pallas_call | solution.py:61
  10.0 5.7 %all-to-all-start = ((bf16[8,96,512]{2,1,0:T(8,128)(2,1)}), bf16[8,96,512]{2,1,0:T(8,128)(2,1)S(1)}, u32[]{:S(2)}, u32[]{:S(2)}) async-start(bf16[8,96,512]{2,1,0:T(8,128)(2,1)} %shard_map.140), calls=%async_computation | async-start | bytes 1572864 | tf_op jit(solution)/shard_map/all_to_all | solution.py:180
  15.6 0.0 copy-done
  15.6 0.3 collective-permute-start.5
  15.9 1.8 %collective-permute-start.4 = (bf16[128,1536]{1,0:T(8,128)(2,1)S(1)}, bf16[128,1536]{1,0:T(8,128)(2,1)S(1)}, u32[]{:S(2)}, u32[]{:S(2)}) collective-permute-start(bf16[128,1536]{1,0:T(8,128)(2,1)S(1)} %copy-done), channel_id=1, source_target_pairs={{0,192},{64,0},{128,64},{192,128},{1,193},{65,1},{129,65},{193,129... | collective-permute-start | bytes 1179656 | tf_op jit(solution)/shard_map/ppermute | solution.py:104
  17.7 8.5 %collective-permute-done.5.refs_4_ = bf16[128,1536]{1,0:T(8,128)(2,1)S(1)} collective-permute-done((bf16[128,1536]{1,0:T(8,128)(2,1)S(1)}, bf16[128,1536]{1,0:T(8,128)(2,1)S(1)}, u32[]{:S(2)}, u32[]{:S(2)}) %collective-permute-start.5) | collective-permute-done | bytes 393248 | tf_op jit(solution)/shard_map/ppermute | solution.py:103
  26.3 1.6 %collective-permute-start.6 = (bf16[128,768]{1,0:T(8,128)(2,1)S(1)}, bf16[128,768]{1,0:T(8,128)(2,1)S(1)}, u32[]{:S(2)}, u32[]{:S(2)}) collective-permute-start(bf16[128,768]{1,0:T(8,128)(2,1)S(1)} %slice.28), channel_id=1, source_target_pairs={{0,64},{64,128},{128,192},{192,0},{1,65},{65,129},{129,193},{193,1... | collective-permute-start | bytes 589832 | tf_op jit(solution)/shard_map/ppermute | solution.py:108
  27.9 0.6 all-to-all-done.got
  28.5 0.0 copy-done.2
  28.5 0.4 shard_map.141
  29.0 0.7 collective-permute-start
  29.6 0.1 collective-permute-start.8
  29.7 0.0 collective-permute-done.4.refs_1_
  29.8 0.8 %collective-permute-start.7 = (bf16[128,768]{1,0:T(8,128)(2,1)S(1)}, bf16[128,768]{1,0:T(8,128)(2,1)S(1)}, u32[]{:S(2)}, u32[]{:S(2)}) collective-permute-start(bf16[128,768]{1,0:T(8,128)(2,1)S(1)} %slice.29), channel_id=1, source_target_pairs={{0,192},{64,0},{128,64},{192,128},{1,193},{65,1},{129,65},{193,129... | collective-permute-start | bytes 589832 | tf_op jit(solution)/shard_map/ppermute | solution.py:109
  30.6 0.2 collective-permute-start.12
  30.8 1.3 %collective-permute-done.6.refs_2_ = bf16[128,768]{1,0:T(8,128)(2,1)S(1)} collective-permute-done((bf16[128,768]{1,0:T(8,128)(2,1)S(1)}, bf16[128,768]{1,0:T(8,128)(2,1)S(1)}, u32[]{:S(2)}, u32[]{:S(2)}) %collective-permute-start.6) | collective-permute-done | bytes 196640 | tf_op jit(solution)/shard_map/ppermute | solution.py:108
  32.1 0.0 collective-permute-start.9
  32.1 0.0 collective-permute-done
  32.1 0.5 collective-permute-start.10
  32.6 0.0 copy-start.1
  32.6 0.0 collective-permute-done.8.refs_5_
  32.6 6.4 %collective-permute-start.2 = (bf16[16,1536]{1,0:T(8,128)(2,1)S(1)}, bf16[16,1536]{1,0:T(8,128)(2,1)S(1)}, u32[]{:S(2)}, u32[]{:S(2)}) collective-permute-start(bf16[16,1536]{1,0:T(8,128)(2,1)S(1)} %slice_add_fusion.s0), channel_id=1, source_target_pairs={{0,32},{16,48},{32,0},{48,16},{1,33},{17,49},{33,1},{49,17},{2,34}... | collective-permute-start | bytes 147464 | tf_op jit(solution)/shard_map/ppermute | solution.py:112
  39.0 0.0 collective-permute-done.7.refs_3_
  39.0 0.0 collective-permute-start.11
  39.0 0.0 collective-permute-done.10.refs_7_
  39.0 4.7 %collective-permute-start.1 = (bf16[16,1536]{1,0:T(8,128)(2,1)S(1)}, bf16[16,1536]{1,0:T(8,128)(2,1)S(1)}, u32[]{:S(2)}, u32[]{:S(2)}) collective-permute-start(bf16[16,1536]{1,0:T(8,128)(2,1)S(1)} %slice_add_fusion.s0), channel_id=1, source_target_pairs={{0,48},{16,0},{32,16},{48,32},{1,49},{17,1},{33,17},{49,33},{2,50}... | collective-permute-start | bytes 147464 | tf_op jit(solution)/shard_map/ppermute | solution.py:104
  43.8 0.0 collective-permute-done.2
  43.8 0.6 collective-permute-start.3
  44.4 0.0 collective-permute-done.11.refs_8_
  44.4 0.0 collective-permute-done.12.refs_9_
  44.4 0.0 collective-permute-done.9.refs_6_
  44.4 2.1 %collective-permute-done.1.s1 = bf16[16,1536]{1,0:T(8,128)(2,1)S(1)} collective-permute-done((bf16[16,1536]{1,0:T(8,128)(2,1)S(1)}, bf16[16,1536]{1,0:T(8,128)(2,1)S(1)}, u32[]{:S(2)}, u32[]{:S(2)}) %collective-permute-start.1) | collective-permute-done | bytes 49184 | tf_op jit(solution)/shard_map/ppermute | solution.py:104
  46.5 3.5 %collective-permute-done.3.s3 = bf16[16,1536]{1,0:T(8,128)(2,1)S(1)} collective-permute-done((bf16[16,1536]{1,0:T(8,128)(2,1)S(1)}, bf16[16,1536]{1,0:T(8,128)(2,1)S(1)}, u32[]{:S(2)}, u32[]{:S(2)}) %collective-permute-start.3) | collective-permute-done | bytes 49184 | tf_op jit(solution)/shard_map/ppermute | solution.py:103
  50.0 1.2 %shard_map.142 = bf16[4,8,16,256]{3,2,1,0:T(8,128)(2,1)S(1)} custom-call(bf16[16,1536]{1,0:T(8,128)(2,1)S(1)} %slice_add_fusion.s0, bf16[16,1536]{1,0:T(8,128)(2,1)S(1)} %collective-permute-done.1.s1, bf16[16,768]{1,0:T(8,128)(2,1)S(1)} %get-tuple-element.3.s2a, bf16[16,768]{1,0:T(8,128)(2,1)S(1)} %get-tuple-element.2.s2b, ...), custom_call_target="tpu_custom_call" | custom-call | tf_op jit(solution)/shard_map/pallas_call | solution.py:189
  51.2 21.2 %all_to_all.10 = bf16[32,16,256]{2,1,0:T(8,128)(2,1)S(1)} all-to-all(bf16[32,16,256]{2,1,0:T(8,128)(2,1)S(1)} %bitcast.8), channel_id=1, replica_groups=mesh['y'=4,'zhh'=2,'zhl'=2,'core'=2,'tensor'=8] {'zhh','zhl','tensor'}, dimensions={0} | all-to-all | bytes 524288 | tf_op jit(solution)/shard_map/all_to_all | solution.py:194
  72.4 0.6 shard_map.143
  73.0 0.0 copy-done.1
  (7 shorter events, 0.1 us)
Async XLA Ops:
  0.6 15.0 %copy-start = (bf16[128,1536]{1,0:T(8,128)(2,1)S(1)}, bf16[128,1536]{1,0:T(8,128)(2,1)}, u32[]{:S(2)}) copy-start(bf16[128,1536]{1,0:T(8,128)(2,1)} %refs_0_.1) | copy-start | bytes 1179652
  0.6 27.9 %copy-start.2 = (s32[1,512]{1,0:T(1,128)S(1)}, s32[1,512]{1,0:T(1,128)}, u32[]{:S(2)}) copy-start(s32[1,512]{1,0:T(1,128)} %ids.1) | copy-start | bytes 6148
  10.0 18.6 %all-to-all-start = ((bf16[8,96,512]{2,1,0:T(8,128)(2,1)}), bf16[8,96,512]{2,1,0:T(8,128)(2,1)S(1)}, u32[]{:S(2)}, u32[]{:S(2)}) async-start(bf16[8,96,512]{2,1,0:T(8,128)(2,1)} %shard_map.140), calls=%async_computation | async-start | bytes 1572864 | tf_op jit(solution)/shard_map/all_to_all | solution.py:180
  15.6 10.7 %collective-permute-start.5 = (bf16[128,1536]{1,0:T(8,128)(2,1)S(1)}, bf16[128,1536]{1,0:T(8,128)(2,1)S(1)}, u32[]{:S(2)}, u32[]{:S(2)}) collective-permute-start(bf16[128,1536]{1,0:T(8,128)(2,1)S(1)} %copy-done), channel_id=1, source_target_pairs={{0,64},{64,128},{128,192},{192,0},{1,65},{65,129},{129,193},{193,1... | collective-permute-start | bytes 1179656 | tf_op jit(solution)/shard_map/ppermute | solution.py:103
  15.9 13.8 %collective-permute-start.4 = (bf16[128,1536]{1,0:T(8,128)(2,1)S(1)}, bf16[128,1536]{1,0:T(8,128)(2,1)S(1)}, u32[]{:S(2)}, u32[]{:S(2)}) collective-permute-start(bf16[128,1536]{1,0:T(8,128)(2,1)S(1)} %copy-done), channel_id=1, source_target_pairs={{0,192},{64,0},{128,64},{192,128},{1,193},{65,1},{129,65},{193,129... | collective-permute-start | bytes 1179656 | tf_op jit(solution)/shard_map/ppermute | solution.py:104
  26.3 5.7 %collective-permute-start.6 = (bf16[128,768]{1,0:T(8,128)(2,1)S(1)}, bf16[128,768]{1,0:T(8,128)(2,1)S(1)}, u32[]{:S(2)}, u32[]{:S(2)}) collective-permute-start(bf16[128,768]{1,0:T(8,128)(2,1)S(1)} %slice.28), channel_id=1, source_target_pairs={{0,64},{64,128},{128,192},{192,0},{1,65},{65,129},{129,193},{193,1... | collective-permute-start | bytes 589832 | tf_op jit(solution)/shard_map/ppermute | solution.py:108
  29.0 3.1 %collective-permute-start = (bf16[16,512]{1,0:T(8,128)(2,1)S(1)}, bf16[16,512]{1,0:T(8,128)(2,1)S(1)}, u32[]{:S(2)}, u32[]{:S(2)}) collective-permute-start(bf16[16,512]{1,0:T(8,128)(2,1)S(1)} %slice.25), channel_id=1, source_target_pairs={{3,2},{4,5},{11,10},{12,13},{19,18},{20,21},{27,26},{28,29},{35,34... | collective-permute-start | bytes 49160 | tf_op jit(solution)/shard_map/ppermute | solution.py:183
  29.6 3.0 %collective-permute-start.8 = (bf16[128,1536]{1,0:T(8,128)(2,1)S(1)}, bf16[128,1536]{1,0:T(8,128)(2,1)S(1)}, u32[]{:S(2)}, u32[]{:S(2)}) collective-permute-start(bf16[128,1536]{1,0:T(8,128)(2,1)S(1)} %copy-done), channel_id=1, source_target_pairs={{0,8},{8,0},{1,9},{9,1},{2,10},{10,2},{3,11},{11,3},{4,12},{12,4},... | collective-permute-start | bytes 1179656 | tf_op jit(solution)/shard_map/ppermute | solution.py:178
  29.8 9.2 %collective-permute-start.7 = (bf16[128,768]{1,0:T(8,128)(2,1)S(1)}, bf16[128,768]{1,0:T(8,128)(2,1)S(1)}, u32[]{:S(2)}, u32[]{:S(2)}) collective-permute-start(bf16[128,768]{1,0:T(8,128)(2,1)S(1)} %slice.29), channel_id=1, source_target_pairs={{0,192},{64,0},{128,64},{192,128},{1,193},{65,1},{129,65},{193,129... | collective-permute-start | bytes 589832 | tf_op jit(solution)/shard_map/ppermute | solution.py:109
  30.6 13.8 %collective-permute-start.12 = (bf16[128,1536]{1,0:T(8,128)(2,1)S(1)}, bf16[128,1536]{1,0:T(8,128)(2,1)S(1)}, u32[]{:S(2)}, u32[]{:S(2)}) collective-permute-start(bf16[128,1536]{1,0:T(8,128)(2,1)S(1)} %collective-permute-done.5.refs_4_), channel_id=1, source_target_pairs={{0,8},{8,0},{1,9},{9,1},{2,10},{10,2},{3,11},{11,3},{4,12},{12,4},... | collective-permute-start | bytes 1179656 | tf_op jit(solution)/shard_map/ppermute | solution.py:178
  32.1 12.3 %collective-permute-start.9 = (bf16[128,1536]{1,0:T(8,128)(2,1)S(1)}, bf16[128,1536]{1,0:T(8,128)(2,1)S(1)}, u32[]{:S(2)}, u32[]{:S(2)}) collective-permute-start(bf16[128,1536]{1,0:T(8,128)(2,1)S(1)} %collective-permute-done.4.refs_1_), channel_id=1, source_target_pairs={{0,8},{8,0},{1,9},{9,1},{2,10},{10,2},{3,11},{11,3},{4,12},{12,4},... | collective-permute-start | bytes 1179656 | tf_op jit(solution)/shard_map/ppermute | solution.py:178
  32.1 7.0 %collective-permute-start.10 = (bf16[128,768]{1,0:T(8,128)(2,1)S(1)}, bf16[128,768]{1,0:T(8,128)(2,1)S(1)}, u32[]{:S(2)}, u32[]{:S(2)}) collective-permute-start(bf16[128,768]{1,0:T(8,128)(2,1)S(1)} %collective-permute-done.6.refs_2_), channel_id=1, source_target_pairs={{0,8},{8,0},{1,9},{9,1},{2,10},{10,2},{3,11},{11,3},{4,12},{12,4},... | collective-permute-start | bytes 589832 | tf_op jit(solution)/shard_map/ppermute | solution.py:178
  32.6 40.4 %copy-start.1 = (bf16[16,1536]{1,0:T(8,128)(2,1)}, bf16[16,1536]{1,0:T(8,128)(2,1)S(1)}, u32[]{:S(2)}) copy-start(bf16[16,1536]{1,0:T(8,128)(2,1)S(1)} %slice_add_fusion.s0) | copy-start | bytes 147460
  32.6 11.1 %collective-permute-start.2 = (bf16[16,1536]{1,0:T(8,128)(2,1)S(1)}, bf16[16,1536]{1,0:T(8,128)(2,1)S(1)}, u32[]{:S(2)}, u32[]{:S(2)}) collective-permute-start(bf16[16,1536]{1,0:T(8,128)(2,1)S(1)} %slice_add_fusion.s0), channel_id=1, source_target_pairs={{0,32},{16,48},{32,0},{48,16},{1,33},{17,49},{33,1},{49,17},{2,34}... | collective-permute-start | bytes 147464 | tf_op jit(solution)/shard_map/ppermute | solution.py:112
  39.0 5.3 %collective-permute-start.11 = (bf16[128,768]{1,0:T(8,128)(2,1)S(1)}, bf16[128,768]{1,0:T(8,128)(2,1)S(1)}, u32[]{:S(2)}, u32[]{:S(2)}) collective-permute-start(bf16[128,768]{1,0:T(8,128)(2,1)S(1)} %collective-permute-done.7.refs_3_), channel_id=1, source_target_pairs={{0,8},{8,0},{1,9},{9,1},{2,10},{10,2},{3,11},{11,3},{4,12},{12,4},... | collective-permute-start | bytes 589832 | tf_op jit(solution)/shard_map/ppermute | solution.py:178
  39.0 7.5 %collective-permute-start.1 = (bf16[16,1536]{1,0:T(8,128)(2,1)S(1)}, bf16[16,1536]{1,0:T(8,128)(2,1)S(1)}, u32[]{:S(2)}, u32[]{:S(2)}) collective-permute-start(bf16[16,1536]{1,0:T(8,128)(2,1)S(1)} %slice_add_fusion.s0), channel_id=1, source_target_pairs={{0,48},{16,0},{32,16},{48,32},{1,49},{17,1},{33,17},{49,33},{2,50}... | collective-permute-start | bytes 147464 | tf_op jit(solution)/shard_map/ppermute | solution.py:104
  43.8 6.2 %collective-permute-start.3 = (bf16[16,1536]{1,0:T(8,128)(2,1)S(1)}, bf16[16,1536]{1,0:T(8,128)(2,1)S(1)}, u32[]{:S(2)}, u32[]{:S(2)}) collective-permute-start(bf16[16,1536]{1,0:T(8,128)(2,1)S(1)} %slice_add_fusion.s0), channel_id=1, source_target_pairs={{0,16},{16,32},{32,48},{48,0},{1,17},{17,33},{33,49},{49,1},{2,18}... | collective-permute-start | bytes 147464 | tf_op jit(solution)/shard_map/ppermute | solution.py:103

commit v3 on v2

--- a/solution.py
+++ b/solution.py
@@ -16,7 +16,6 @@
 PIECE = SLOTS + RANK
 DP = ("y", "zhh", "zhl", "core")
 S_AXES = ("zhh", "zhl")
-Q_FAR = "relay"
 VMEM = 60 << 20
 
 Y_RUNS = (
@@ -32,15 +31,27 @@
 X_OF = (0, 0, 0, 1, 1, 2, 2, 2)
 
 
-def project_kernel(gg, gu, go, li, ha, wgg, wgu, wgo, wgi, wui, wha, out):
-    def dot(a, w):
-        return lax.dot_general(a[...], w[...], (((1,), (1,)), ((), ())), preferred_element_type=jnp.float32)
-
-    gate_up = jnp.concatenate([dot(gg, wgg), dot(gu, wgu)], axis=1).T
-    down = jnp.concatenate([dot(go, wgo), dot(ha, wha)], axis=1).T
-    x_gate_up = jnp.concatenate([dot(li, wgi), dot(li, wui)], axis=1).T.astype(jnp.bfloat16)
-    y_t = jnp.concatenate([gate_up, down[:RANK]], axis=0)
-    x_t = (x_gate_up[:RANK], x_gate_up[RANK:], down[RANK:].astype(jnp.bfloat16))
+def project_kernel(*refs):
+    count = len(refs) // 2 - 1
+    ins, out, held, sems = refs[:count], refs[count], refs[count + 1 : -1], refs[-1]
+    copies = [pltpu.make_async_copy(ins[i], held[i], sems.at[i]) for i in range(count)]
+    for copy in copies:
+        copy.start()
+
+    def dot(first, last):
+        for copy in copies[first:last]:
+            copy.wait()
+        weight = [held[i][...] for i in range(first, last - 1)]
+        weight = weight[0] if len(weight) == 1 else jnp.concatenate(weight, axis=0)
+        return lax.dot_general(
+            weight, held[last - 1][...], (((1,), (1,)), ((), ())), preferred_element_type=jnp.float32
+        )
+
+    gate, up = dot(0, 2), dot(2, 4)
+    x_down = dot(4, 6).astype(jnp.bfloat16)
+    y_t = jnp.concatenate([gate, up, dot(6, 8)], axis=0)
+    x_gate_up = dot(8, 11).astype(jnp.bfloat16)
+    x_t = (x_gate_up[:RANK], x_gate_up[RANK:], x_down)
     zeros = jnp.zeros((EXTRA, y_t.shape[1]), jnp.float32)
     for t in range(TENSOR):
         runs = [zeros if run is None else y_t[run[0] : run[1]] for run in Y_RUNS[t]]
@@ -48,25 +59,18 @@
         out[t, SLOTS:, :] = x_t[X_OF[t]]
 
 
-def project(acts, weights):
-    tok = acts[0].shape[0]
-    step = 128
-
-    def rows(a):
-        return pl.BlockSpec((step, a.shape[1]), lambda i: (i, 0))
-
-    def whole(a):
-        return pl.BlockSpec(a.shape, lambda i: (0, 0))
-
+def project(*operands):
+    tok = operands[1].shape[0]
     return pl.pallas_call(
         project_kernel,
-        grid=(tok // step,),
-        in_specs=[rows(a) for a in acts] + [whole(w) for w in weights],
-        out_specs=pl.BlockSpec((TENSOR, PIECE, step), lambda i: (0, 0, i)),
+        in_specs=[pl.BlockSpec(memory_space=pl.ANY)] * len(operands),
+        out_specs=pl.BlockSpec(memory_space=pltpu.VMEM),
         out_shape=jax.ShapeDtypeStruct((TENSOR, PIECE, tok), jnp.bfloat16),
+        scratch_shapes=[pltpu.VMEM(a.shape, a.dtype) for a in operands]
+        + [pltpu.SemaphoreType.DMA((len(operands),))],
         compiler_params=pltpu.CompilerParams(vmem_limit_bytes=VMEM),
         cost_estimate=pl.CostEstimate(flops=10**9, bytes_accessed=15 << 20, transcendentals=0),
-    )(*acts, *weights)
+    )(*operands)
 
 
 def sketch_kernel(got, ids, out):
@@ -114,32 +118,20 @@
     return x, after, far, before
 
 
-def score_kernel(s0, s1, s2a, s2b, s3, *refs):
-    pieces, out = refs[:-1], refs[-1]
+def score_kernel(sketches, queries, out):
     y, core = lax.axis_index("y"), lax.axis_index("core")
     zhh = lax.axis_index("zhh")
-    zh = zhh * 2 + lax.axis_index("zhl")
-    far = jnp.concatenate([s2a[...], s2b[...]], axis=1)
-    group = jnp.concatenate([s0[...], s1[...], far, s3[...]], axis=0)
+    group = sketches[...].reshape(4 * EX_DEV, ROWS * RANK)
     out[...] = jnp.zeros(out.shape, out.dtype)
-    half = group.shape[1] // 2
-    dims = (((1,), (1,)), ((), ()))
-
-    def dot(left, right):
-        return lax.dot_general(left, right, dims, preferred_element_type=jnp.float32)
-
     for c in range(2):
-        q0, q1, q2a, q2b, q3 = pieces[5 * c : 5 * c + 5]
         lane = pl.multiple_of(lax.rem(core + c, 2) * 128, 128)
-        for r, q in enumerate((q0, q1, (q2a, q2b), q3)):
-            if r == 2:
-                part = dot(group[:, :half], q2a[...]) + dot(group[:, half:], q2b[...])
-            else:
-                part = dot(group, q[...])
-            part = part.astype(jnp.bfloat16)
+        for r in range(4):
+            part = lax.dot_general(
+                group, queries[4 * c + r], (((1,), (1,)), ((), ())), preferred_element_type=jnp.float32
+            ).astype(jnp.bfloat16)
             slot = lax.rem(y + r, 4) * 2 + zhh
             for z in range(4):
-                out[lax.rem(zh + z, 4), slot, :, pl.ds(lane, 128)] = part[z * EX_DEV : (z + 1) * EX_DEV]
+                out[z, slot, :, pl.ds(lane, 128)] = part[z * EX_DEV : (z + 1) * EX_DEV]
 
 
 def finish_kernel(back, out):
@@ -172,12 +164,21 @@
     query_sketches,
 ):
     t = lax.axis_index("tensor")
-    acts = (grad_gate, grad_up, grad_output, layer_input, hidden_act)
-    weights = (proj_gate_out, proj_up_out, proj_down_out, proj_gate_in, proj_up_in, proj_down_in)
-    queries = flat(around(query_sketches, "y", Q_FAR == "relay"))
+    before, after = (lax.ppermute(query_sketches, "y", ring("y", shift)) for shift in (1, -1))
+    send = project(
+        proj_gate_out.T, grad_gate, proj_up_out.T, grad_up, proj_down_in.T, hidden_act,
+        proj_down_out.T, grad_output, proj_gate_in.T, proj_up_in.T, layer_input,
+    )
+    send, before, after = lax.optimization_barrier((send, before, after))
+    half = query_sketches.shape[1] // 2
+    far = (
+        lax.ppermute(before[:, :half], "y", ring("y", 1)),
+        lax.ppermute(after[:, half:], "y", ring("y", -1)),
+    )
+    queries = flat((query_sketches, after, far, before))
     others = tuple(lax.ppermute(q, "core", ring("core", 1)) for q in queries)
-    send = project(acts, tuple(w.T for w in weights))
     got = lax.all_to_all(send, "tensor", 0, 0, tiled=True)
+    got, queries, others = lax.optimization_barrier((got, queries, others))
     wide = sketch_of(got, example_ids)
     main, extra = wide[:, : ROWS * RANK], wide[:, ROWS * RANK :]
     moved = lax.ppermute(extra, "tensor", [(3, 2), (4, 5)])
@@ -185,12 +186,17 @@
     place = jnp.concatenate([jnp.where(t == 5, moved, none), none, jnp.where(t == 2, moved, none)], axis=1)
     sketch = main + place
 
-    group = flat(around(sketch, S_AXES, False))
+    sent, queries, others = lax.optimization_barrier((sketch, queries, others))
+    group = lax.all_to_all(jnp.broadcast_to(sent, (4,) + sketch.shape), S_AXES, 0, 0, tiled=True)
+    held = []
+    for own, after, low, high, before in (queries, others):
+        held += [own, after, jnp.concatenate([low, high], axis=1), before]
+    held = jnp.stack(held)
     partial = pl.pallas_call(
         score_kernel,
         out_shape=jax.ShapeDtypeStruct((4, TENSOR, EX_DEV, 256), jnp.bfloat16),
         compiler_params=pltpu.CompilerParams(vmem_limit_bytes=32 << 20),
-    )(*group, *queries, *others)
+    )(group, held)
     back = lax.all_to_all(partial.reshape(4 * TENSOR, EX_DEV, 256), S_AXES + ("tensor",), 0, 0, tiled=True)
     scores = pl.pallas_call(
         finish_kernel,

time: 74.4 us -> 72.8 us (0.978); the launches traced: 73 us -> 72.4 us
  local copies, waits for them, and re-layouts: 0.06 us -> 4.61 us
  starting transfers between devices: 23.3 us -> 18.8 us
  Pallas kernels: 11.6 us -> 10.1 us
  other arithmetic: 0.03 us -> 1.11 us
    ppermute x7 -> x4, starting transfers between devices: 16.2 us -> 4.28 us  [the longest x2 2.1 us: per_device(): lax.ppermute(query_sketches, 'y', ring('y', shift))]
    all_to_all x0 -> x1, starting transfers between devices: none -> 7.56 us  [per_device(): lax.all_to_all(jnp.broadcast_to(sent, (4,) + sketch.shape), S_AXES, 0, 0,...]
    ppermute x7 -> x4, waiting for transfers between devices: 15.4 us -> 8.45 us  [the longest x1 4.67 us: per_device(): lax.ppermute(before[:, :half], 'y', ring('y', 1))]
    all_to_all x0 -> x1, waiting for transfers between devices: none -> 4.41 us  [per_device(): lax.all_to_all(jnp.broadcast_to(sent, (4,) + sketch.shape), S_AXES, 0, 0,...]
    unnamed x6 -> x37, local copies, waits for them, and re-layouts: 0.02 us -> 3.84 us
    pallas_call x1, Pallas kernels: 9.32 us -> 7.86 us  [project(): pl.pallas_call(project_kernel, in_specs=[pl.BlockSpec(memory_space=pl.ANY...]
    ppermute x5, waiting for transfers between devices: 0.01 us -> 1.43 us  [per_device(): others = tuple((lax.ppermute(q, 'core', ring('core', 1)) for q in queries))]
    unnamed x0 -> x2, other arithmetic: none -> 1.08 us
  transfers between devices with their start and end apart: 14 -> 12, of which waited for: 5 -> 8; matrix products, arithmetic and copies ran while one was open for 0% -> 6% of each run, Pallas kernels for 1% -> 11%
where the time goes in v3:
time: 72.8 us; the launch traced here: 72.4 us
  blocking collectives  21 us (29%)
  starting transfers between devices  18.8 us (26%)
  waiting for transfers between devices  15.9 us (22%)
  Pallas kernels  10.1 us (14%)
  local copies, waits for them, and re-layouts  4.61 us (6%)
  other arithmetic  1.11 us (2%)
  between operations  0.92 us (1%)
    all_to_all x1, blocking collectives, per_device(): lax.all_to_all(partial.reshape(4 * TENSOR, EX_DEV, 256), S_AXES + ('tenso...  21 us
    pallas_call x1, Pallas kernels, project(): pl.pallas_call(project_kernel, in_specs=[pl.BlockSpec(memory_space=pl.ANY...  7.86 us
    all_to_all x1, starting transfers between devices, per_device(): lax.all_to_all(jnp.broadcast_to(sent, (4,) + sketch.shape), S_AXES, 0, 0,...  7.56 us
    all_to_all x1, starting transfers between devices, per_device(): got = lax.all_to_all(send, 'tensor', 0, 0, tiled=True)  5.65 us
    ppermute x1, waiting for transfers between devices, per_device(): lax.ppermute(before[:, :half], 'y', ring('y', 1))  4.67 us
    all_to_all x1, waiting for transfers between devices, per_device(): lax.all_to_all(jnp.broadcast_to(sent, (4,) + sketch.shape), S_AXES, 0, 0,...  4.41 us
    unnamed x37, local copies, waits for them, and re-layouts  3.84 us
    ppermute x2, waiting for transfers between devices, per_device(): lax.ppermute(query_sketches, 'y', ring('y', shift))  2.46 us
  transfers between devices with their start and end apart: 12, of which 8 were waited for; matrix products, arithmetic and copies ran while one was open for 6% of the time, Pallas kernels for 11%

profile of v3, /device:TPU:24, one launch (start us, length us, event | category | flops | bytes accessed | tf_op | source)
XLA Modules:
  0.0 72.4 jit_solution(15417861748765313239)
XLA Ops:
  0.6 2.0 %collective-permute-start = (bf16[128,1536]{1,0:T(8,128)(2,1)}, bf16[128,1536]{1,0:T(8,128)(2,1)S(1)}, u32[]{:S(2)}, u32[]{:S(2)}) collective-permute-start(bf16[128,1536]{1,0:T(8,128)(2,1)} %param.25), channel_id=1, source_target_pairs={{0,64},{64,128},{128,192},{192,0},{1,65},{65,129},{129,193},{193,1... | collective-permute-start | bytes 1179656 | tf_op jit(solution)/shard_map/ppermute | solution.py:167
  2.7 0.1 collective-permute-start.1
  2.7 7.9 %shard_map.140 = bf16[8,96,512]{2,1,0:T(8,128)(2,1)} custom-call(bf16[64,3584]{1,0:T(8,128)(2,1)} %bitcast.30, bf16[512,3584]{1,0:T(8,128)(2,1)} %refs_1_.1, bf16[64,3584]{1,0:T(8,128)(2,1)} %bitcast.31, bf16[512,3584]{1,0:T(8,128)(2,1)} %refs_3_.1, bf16[64,3584]{1,0:T(8,128)(2,1)} %bitcast.32, bf16[512,3584]{1,0:T(8,128)(2,1)} %refs_5_.1, ...), custom_call_target="tpu_custom_call" | custom-call | flops 1000000000 | bytes 15728640 | tf_op jit(solution)/shard_map/pallas_call | solution.py:64
  10.6 1.2 %collective-permute-done = bf16[128,1536]{1,0:T(8,128)(2,1)S(1)} collective-permute-done((bf16[128,1536]{1,0:T(8,128)(2,1)}, bf16[128,1536]{1,0:T(8,128)(2,1)S(1)}, u32[]{:S(2)}, u32[]{:S(2)}) %collective-permute-start) | collective-permute-done | bytes 393248 | tf_op jit(solution)/shard_map/ppermute | solution.py:167
  11.8 1.3 %collective-permute-done.1 = bf16[128,1536]{1,0:T(8,128)(2,1)S(1)} collective-permute-done((bf16[128,1536]{1,0:T(8,128)(2,1)}, bf16[128,1536]{1,0:T(8,128)(2,1)S(1)}, u32[]{:S(2)}, u32[]{:S(2)}) %collective-permute-start.1) | collective-permute-done | bytes 393248 | tf_op jit(solution)/shard_map/ppermute | solution.py:167
  13.1 5.7 %all-to-all-start = ((bf16[8,96,512]{2,1,0:T(8,128)(2,1)}), bf16[8,96,512]{2,1,0:T(8,128)(2,1)S(1)}, u32[]{:S(2)}, u32[]{:S(2)}) async-start(bf16[8,96,512]{2,1,0:T(8,128)(2,1)} %shard_map.140), calls=%async_computation | async-start | bytes 1572864 | tf_op jit(solution)/shard_map/all_to_all | solution.py:180
  18.7 0.0 copy-done.3
  18.7 0.1 collective-permute-start.4
  18.9 0.3 collective-permute-start.2
  19.2 1.9 %collective-permute-start.3 = (bf16[128,768]{1,0:T(8,128)(2,1)S(1)}, bf16[128,768]{1,0:T(8,128)(2,1)S(1)}, u32[]{:S(2)}, u32[]{:S(2)}) collective-permute-start(bf16[128,768]{1,0:T(8,128)(2,1)S(1)} %slice.13), channel_id=1, source_target_pairs={{0,192},{64,0},{128,64},{192,128},{1,193},{65,1},{129,65},{193,129... | collective-permute-start | bytes 589832 | tf_op jit(solution)/shard_map/ppermute | solution.py:176
  21.1 0.0 collective-permute-start.5
  21.1 0.5 collective-permute-start.8
  21.6 4.7 %collective-permute-done.2 = bf16[128,768]{1,0:T(8,128)(2,1)S(1)} collective-permute-done((bf16[128,768]{1,0:T(8,128)(2,1)S(1)}, bf16[128,768]{1,0:T(8,128)(2,1)S(1)}, u32[]{:S(2)}, u32[]{:S(2)}) %collective-permute-start.2) | collective-permute-done | bytes 196640 | tf_op jit(solution)/shard_map/ppermute | solution.py:175
  26.2 0.0 collective-permute-start.6
  26.2 1.3 %collective-permute-done.3 = bf16[128,768]{1,0:T(8,128)(2,1)S(1)} collective-permute-done((bf16[128,768]{1,0:T(8,128)(2,1)S(1)}, bf16[128,768]{1,0:T(8,128)(2,1)S(1)}, u32[]{:S(2)}, u32[]{:S(2)}) %collective-permute-start.3) | collective-permute-done | bytes 196640 | tf_op jit(solution)/shard_map/ppermute | solution.py:176
  27.6 0.0 collective-permute-start.7
  27.6 0.0 collective-permute-done.4
  27.6 0.0 copy-start.4
  27.6 0.1 collective-permute-done.6
  27.7 1.3 %collective-permute-done.7 = bf16[128,768]{1,0:T(8,128)(2,1)S(1)} collective-permute-done((bf16[128,768]{1,0:T(8,128)(2,1)S(1)}, bf16[128,768]{1,0:T(8,128)(2,1)S(1)}, u32[]{:S(2)}, u32[]{:S(2)}) %collective-permute-start.7) | collective-permute-done | bytes 196640 | tf_op jit(solution)/shard_map/ppermute | solution.py:179
  29.0 0.0 collective-permute-done.5
  29.0 0.0 copy-done.9
  29.0 0.0 copy-done.10
  29.0 0.0 copy-done.11
  29.0 0.0 copy-start.7
  29.0 0.0 collective-permute-done.8
  29.1 0.0 copy-done.1
  29.1 0.0 copy-start.5
  29.1 1.6 %all-to-all-done.got = bf16[8,96,512]{2,1,0:T(8,128)(2,1)S(1)} async-done(((bf16[8,96,512]{2,1,0:T(8,128)(2,1)}), bf16[8,96,512]{2,1,0:T(8,128)(2,1)S(1)}, u32[]{:S(2)}, u32[]{:S(2)}) %all-to-all-start) | async-done | bytes 786464 | tf_op jit(solution)/shard_map/all_to_all | solution.py:180
  30.7 0.0 copy-done
  30.7 0.4 shard_map.141
  31.1 0.7 collective-permute-start.9
  31.8 0.0 collective-permute-done.9
  31.8 0.0 copy-done.2
  31.8 0.0 copy-done.4
  31.9 0.0 copy-done.13
  31.9 0.0 copy-start.15
  32.0 0.6 copy-done.15
  32.5 0.7 broadcast_in_dim.7
  33.2 7.6 %all-to-all-start.1 = ((bf16[4,16,1536]{2,1,0:T(8,128)(2,1)}), bf16[4,16,1536]{2,1,0:T(8,128)(2,1)S(1)}, u32[]{:S(2)}, u32[]{:S(2)}) async-start(bf16[4,16,1536]{2,1,0:T(8,128)(2,1)} %broadcast_in_dim.7), calls=%async_computation.1 | async-start | bytes 393216 | tf_op jit(solution)/shard_map/all_to_all | solution.py:190
  40.8 1.1 %bitcast_dynamic-update-slice_fusion.4 = bf16[8,128,1536]{2,1,0:T(8,128)(2,1)S(1)} fusion(bf16[8,128,1536]{2,1,0:T(8,128)(2,1)S(1)} %bitcast_dynamic-update-slice_fusion.5, bf16[128,1536]{1,0:T(8,128)(2,1)} %copy-done.2), kind=kLoop, calls=%fused_computation.8 | loop fusion | bytes 786432
  41.9 1.1 %fusion = bf16[8,128,1536]{2,1,0:T(8,128)(2,1)S(1)} fusion(bf16[8,128,1536]{2,1,0:T(8,128)(2,1)S(1)} %bitcast_dynamic-update-slice_fusion.4, bf16[128,768]{1,0:T(8,128)(2,1)} %copy-done.10, bf16[128,768]{1,0:T(8,128)(2,1)} %copy-done.9), kind=kLoop, calls=%fused_computation.1 | loop fusion | flops 786432 | bytes 786432
  43.0 1.0 %bitcast_dynamic-update-slice_fusion.3 = bf16[8,128,1536]{2,1,0:T(8,128)(2,1)S(1)} fusion(bf16[8,128,1536]{2,1,0:T(8,128)(2,1)S(1)} %fusion, bf16[128,1536]{1,0:T(8,128)(2,1)} %copy-done.1), kind=kLoop, calls=%fused_computation.7 | loop fusion | bytes 786432
  44.0 1.0 %bitcast_dynamic-update-slice_fusion.2 = bf16[8,128,1536]{2,1,0:T(8,128)(2,1)S(1)} fusion(bf16[8,128,1536]{2,1,0:T(8,128)(2,1)S(1)} %bitcast_dynamic-update-slice_fusion.3, bf16[128,1536]{1,0:T(8,128)(2,1)} %copy-done.4), kind=kLoop, calls=%fused_computation.6 | loop fusion | bytes 786432
  45.2 4.4 %all-to-all-done.1.sketches = bf16[4,16,1536]{2,1,0:T(8,128)(2,1)S(1)} async-done(((bf16[4,16,1536]{2,1,0:T(8,128)(2,1)}), bf16[4,16,1536]{2,1,0:T(8,128)(2,1)S(1)}, u32[]{:S(2)}, u32[]{:S(2)}) %all-to-all-start.1) | async-done | bytes 196640 | tf_op jit(solution)/shard_map/all_to_all | solution.py:190
  49.6 1.2 %shard_map.142 = bf16[4,8,16,256]{3,2,1,0:T(8,128)(2,1)S(1)} custom-call(bf16[4,16,1536]{2,1,0:T(8,128)(2,1)S(1)} %all-to-all-done.1.sketches, bf16[8,128,1536]{2,1,0:T(8,128)(2,1)S(1)} %bitcast_dynamic-update-slice_fusion.queries), custom_call_target="tpu_custom_call" | custom-call | tf_op jit(solution)/shard_map/pallas_call | solution.py:195
  50.8 21.0 %all_to_all.15 = bf16[32,16,256]{2,1,0:T(8,128)(2,1)S(1)} all-to-all(bf16[32,16,256]{2,1,0:T(8,128)(2,1)S(1)} %bitcast.28), channel_id=1, replica_groups=mesh['y'=4,'zhh'=2,'zhl'=2,'core'=2,'tensor'=8] {'zhh','zhl','tensor'}, dimensions={0} | all-to-all | bytes 524288 | tf_op jit(solution)/shard_map/all_to_all | solution.py:200
  71.8 0.6 shard_map.143
  (28 shorter events, 0.2 us)
Async XLA Ops:
  0.6 11.1 %collective-permute-start = (bf16[128,1536]{1,0:T(8,128)(2,1)}, bf16[128,1536]{1,0:T(8,128)(2,1)S(1)}, u32[]{:S(2)}, u32[]{:S(2)}) collective-permute-start(bf16[128,1536]{1,0:T(8,128)(2,1)} %param.25), channel_id=1, source_target_pairs={{0,64},{64,128},{128,192},{192,0},{1,65},{65,129},{129,193},{193,1... | collective-permute-start | bytes 1179656 | tf_op jit(solution)/shard_map/ppermute | solution.py:167
  2.7 10.4 %collective-permute-start.1 = (bf16[128,1536]{1,0:T(8,128)(2,1)}, bf16[128,1536]{1,0:T(8,128)(2,1)S(1)}, u32[]{:S(2)}, u32[]{:S(2)}) collective-permute-start(bf16[128,1536]{1,0:T(8,128)(2,1)} %param.25), channel_id=1, source_target_pairs={{0,192},{64,0},{128,64},{192,128},{1,193},{65,1},{129,65},{193,129... | collective-permute-start | bytes 1179656 | tf_op jit(solution)/shard_map/ppermute | solution.py:167
  2.7 16.0 %copy-start.3 = (bf16[128,1536]{1,0:T(8,128)(2,1)S(1)}, bf16[128,1536]{1,0:T(8,128)(2,1)}, u32[]{:S(2)}) copy-start(bf16[128,1536]{1,0:T(8,128)(2,1)} %param.25) | copy-start | bytes 1179652
  2.7 27.9 %copy-start = (s32[1,512]{1,0:T(1,128)S(1)}, s32[1,512]{1,0:T(1,128)}, u32[]{:S(2)}) copy-start(s32[1,512]{1,0:T(1,128)} %ids.1) | copy-start | bytes 6148
  11.8 17.3 %copy-start.1 = (bf16[128,1536]{1,0:T(8,128)(2,1)}, bf16[128,1536]{1,0:T(8,128)(2,1)S(1)}, u32[]{:S(2)}) copy-start(bf16[128,1536]{1,0:T(8,128)(2,1)S(1)} %collective-permute-done) | copy-start | bytes 1179652
  13.1 18.8 %copy-start.2 = (bf16[128,1536]{1,0:T(8,128)(2,1)}, bf16[128,1536]{1,0:T(8,128)(2,1)S(1)}, u32[]{:S(2)}) copy-start(bf16[128,1536]{1,0:T(8,128)(2,1)S(1)} %collective-permute-done.1) | copy-start | bytes 1179652
  13.1 17.6 %all-to-all-start = ((bf16[8,96,512]{2,1,0:T(8,128)(2,1)}), bf16[8,96,512]{2,1,0:T(8,128)(2,1)S(1)}, u32[]{:S(2)}, u32[]{:S(2)}) async-start(bf16[8,96,512]{2,1,0:T(8,128)(2,1)} %shard_map.140), calls=%async_computation | async-start | bytes 1572864 | tf_op jit(solution)/shard_map/all_to_all | solution.py:180
  18.7 8.8 %collective-permute-start.4 = (bf16[128,1536]{1,0:T(8,128)(2,1)S(1)}, bf16[128,1536]{1,0:T(8,128)(2,1)S(1)}, u32[]{:S(2)}, u32[]{:S(2)}) collective-permute-start(bf16[128,1536]{1,0:T(8,128)(2,1)S(1)} %copy-done.3), channel_id=1, source_target_pairs={{0,8},{8,0},{1,9},{9,1},{2,10},{10,2},{3,11},{11,3},{4,12},{12,4},... | collective-permute-start | bytes 1179656 | tf_op jit(solution)/shard_map/ppermute | solution.py:179
  18.9 7.4 %collective-permute-start.2 = (bf16[128,768]{1,0:T(8,128)(2,1)S(1)}, bf16[128,768]{1,0:T(8,128)(2,1)S(1)}, u32[]{:S(2)}, u32[]{:S(2)}) collective-permute-start(bf16[128,768]{1,0:T(8,128)(2,1)S(1)} %slice.12), channel_id=1, source_target_pairs={{0,64},{64,128},{128,192},{192,0},{1,65},{65,129},{129,193},{193,1... | collective-permute-start | bytes 589832 | tf_op jit(solution)/shard_map/ppermute | solution.py:175
  19.2 8.4 %collective-permute-start.3 = (bf16[128,768]{1,0:T(8,128)(2,1)S(1)}, bf16[128,768]{1,0:T(8,128)(2,1)S(1)}, u32[]{:S(2)}, u32[]{:S(2)}) collective-permute-start(bf16[128,768]{1,0:T(8,128)(2,1)S(1)} %slice.13), channel_id=1, source_target_pairs={{0,192},{64,0},{128,64},{192,128},{1,193},{65,1},{129,65},{193,129... | collective-permute-start | bytes 589832 | tf_op jit(solution)/shard_map/ppermute | solution.py:176
  21.1 8.0 %collective-permute-start.5 = (bf16[128,1536]{1,0:T(8,128)(2,1)S(1)}, bf16[128,1536]{1,0:T(8,128)(2,1)S(1)}, u32[]{:S(2)}, u32[]{:S(2)}) collective-permute-start(bf16[128,1536]{1,0:T(8,128)(2,1)S(1)} %collective-permute-done.1), channel_id=1, source_target_pairs={{0,8},{8,0},{1,9},{9,1},{2,10},{10,2},{3,11},{11,3},{4,12},{12,4},... | collective-permute-start | bytes 1179656 | tf_op jit(solution)/shard_map/ppermute | solution.py:179
  21.1 8.0 %collective-permute-start.8 = (bf16[128,1536]{1,0:T(8,128)(2,1)S(1)}, bf16[128,1536]{1,0:T(8,128)(2,1)S(1)}, u32[]{:S(2)}, u32[]{:S(2)}) collective-permute-start(bf16[128,1536]{1,0:T(8,128)(2,1)S(1)} %collective-permute-done), channel_id=1, source_target_pairs={{0,8},{8,0},{1,9},{9,1},{2,10},{10,2},{3,11},{11,3},{4,12},{12,4},... | collective-permute-start | bytes 1179656 | tf_op jit(solution)/shard_map/ppermute | solution.py:179
  26.2 2.8 %copy-start.9 = (bf16[128,768]{1,0:T(8,128)(2,1)}, bf16[128,768]{1,0:T(8,128)(2,1)S(1)}, u32[]{:S(2)}) copy-start(bf16[128,768]{1,0:T(8,128)(2,1)S(1)} %collective-permute-done.2) | copy-start | bytes 589828
  26.2 1.4 %collective-permute-start.6 = (bf16[128,768]{1,0:T(8,128)(2,1)S(1)}, bf16[128,768]{1,0:T(8,128)(2,1)S(1)}, u32[]{:S(2)}, u32[]{:S(2)}) collective-permute-start(bf16[128,768]{1,0:T(8,128)(2,1)S(1)} %collective-permute-done.2), channel_id=1, source_target_pairs={{0,8},{8,0},{1,9},{9,1},{2,10},{10,2},{3,11},{11,3},{4,12},{12,4},... | collective-permute-start | bytes 589832 | tf_op jit(solution)/shard_map/ppermute | solution.py:179
  27.6 1.5 %copy-start.10 = (bf16[128,768]{1,0:T(8,128)(2,1)}, bf16[128,768]{1,0:T(8,128)(2,1)S(1)}, u32[]{:S(2)}) copy-start(bf16[128,768]{1,0:T(8,128)(2,1)S(1)} %collective-permute-done.3) | copy-start | bytes 589828
  27.6 1.4 %collective-permute-start.7 = (bf16[128,768]{1,0:T(8,128)(2,1)S(1)}, bf16[128,768]{1,0:T(8,128)(2,1)S(1)}, u32[]{:S(2)}, u32[]{:S(2)}) collective-permute-start(bf16[128,768]{1,0:T(8,128)(2,1)S(1)} %collective-permute-done.3), channel_id=1, source_target_pairs={{0,8},{8,0},{1,9},{9,1},{2,10},{10,2},{3,11},{11,3},{4,12},{12,4},... | collective-permute-start | bytes 589832 | tf_op jit(solution)/shard_map/ppermute | solution.py:179
  27.6 4.3 %copy-start.4 = (bf16[128,1536]{1,0:T(8,128)(2,1)}, bf16[128,1536]{1,0:T(8,128)(2,1)S(1)}, u32[]{:S(2)}) copy-start(bf16[128,1536]{1,0:T(8,128)(2,1)S(1)} %collective-permute-done.4) | copy-start | bytes 1179652
  27.7 1.3 %copy-start.11 = (bf16[128,768]{1,0:T(8,128)(2,1)}, bf16[128,768]{1,0:T(8,128)(2,1)S(1)}, u32[]{:S(2)}) copy-start(bf16[128,768]{1,0:T(8,128)(2,1)S(1)} %collective-permute-done.6) | copy-start | bytes 589828
  29.0 2.8 %copy-start.13 = (bf16[128,768]{1,0:T(8,128)(2,1)}, bf16[128,768]{1,0:T(8,128)(2,1)S(1)}, u32[]{:S(2)}) copy-start(bf16[128,768]{1,0:T(8,128)(2,1)S(1)} %collective-permute-done.7) | copy-start | bytes 589828
  29.0 2.8 %copy-start.7 = (bf16[128,1536]{1,0:T(8,128)(2,1)}, bf16[128,1536]{1,0:T(8,128)(2,1)S(1)}, u32[]{:S(2)}) copy-start(bf16[128,1536]{1,0:T(8,128)(2,1)S(1)} %collective-permute-done.5) | copy-start | bytes 1179652
  29.1 2.8 %copy-start.5 = (bf16[128,1536]{1,0:T(8,128)(2,1)}, bf16[128,1536]{1,0:T(8,128)(2,1)S(1)}, u32[]{:S(2)}) copy-start(bf16[128,1536]{1,0:T(8,128)(2,1)S(1)} %collective-permute-done.8) | copy-start | bytes 1179652
  31.1 0.7 collective-permute-start.9
  31.9 0.6 copy-start.15
  32.5 12.5 %copy-start.12 = (bf16[128,768]{1,0:T(8,128)(2,1)S(1)}, bf16[128,768]{1,0:T(8,128)(2,1)}, u32[]{:S(2)}) copy-start(bf16[128,768]{1,0:T(8,128)(2,1)} %copy-done.11) | copy-start | bytes 589828
  33.2 16.3 %all-to-all-start.1 = ((bf16[4,16,1536]{2,1,0:T(8,128)(2,1)}), bf16[4,16,1536]{2,1,0:T(8,128)(2,1)S(1)}, u32[]{:S(2)}, u32[]{:S(2)}) async-start(bf16[4,16,1536]{2,1,0:T(8,128)(2,1)} %broadcast_in_dim.7), calls=%async_computation.1 | async-start | bytes 393216 | tf_op jit(solution)/shard_map/all_to_all | solution.py:190
  40.8 4.2 %copy-start.8 = (bf16[128,1536]{1,0:T(8,128)(2,1)S(1)}, bf16[128,1536]{1,0:T(8,128)(2,1)}, u32[]{:S(2)}) copy-start(bf16[128,1536]{1,0:T(8,128)(2,1)} %copy-done.7) | copy-start | bytes 1179652
  40.8 4.3 %copy-start.14 = (bf16[128,768]{1,0:T(8,128)(2,1)S(1)}, bf16[128,768]{1,0:T(8,128)(2,1)}, u32[]{:S(2)}) copy-start(bf16[128,768]{1,0:T(8,128)(2,1)} %copy-done.13) | copy-start | bytes 589828
  40.8 4.3 %copy-start.6 = (bf16[128,1536]{1,0:T(8,128)(2,1)S(1)}, bf16[128,1536]{1,0:T(8,128)(2,1)}, u32[]{:S(2)}) copy-start(bf16[128,1536]{1,0:T(8,128)(2,1)} %copy-done.5) | copy-start | bytes 1179652

commit v4 on v3

--- a/solution.py
+++ b/solution.py
@@ -178,7 +178,7 @@
     queries = flat((query_sketches, after, far, before))
     others = tuple(lax.ppermute(q, "core", ring("core", 1)) for q in queries)
     got = lax.all_to_all(send, "tensor", 0, 0, tiled=True)
-    got, queries, others = lax.optimization_barrier((got, queries, others))
+    got, _ = lax.optimization_barrier((got, far))
     wide = sketch_of(got, example_ids)
     main, extra = wide[:, : ROWS * RANK], wide[:, ROWS * RANK :]
     moved = lax.ppermute(extra, "tensor", [(3, 2), (4, 5)])

time: 72.8 us -> 75.7 us (1.040)
  blocking collectives: 21 us -> 17.7 us
  waiting for transfers between devices: 15.9 us -> 18.8 us
  local copies, waits for them, and re-layouts: 4.61 us -> 7.46 us
    all_to_all x1, blocking collectives: 21 us -> 17.7 us  [per_device(): lax.all_to_all(partial.reshape(4 * TENSOR, EX_DEV, 256), S_AXES + ('tenso...]
    all_to_all x1, waiting for transfers between devices: 1.61 us -> 4.67 us  [per_device(): got = lax.all_to_all(send, 'tensor', 0, 0, tiled=True)]
    unnamed x37 -> x33, local copies, waits for them, and re-layouts: 3.84 us -> 5.7 us
    ppermute x1, waiting for transfers between devices: 4.67 us -> 3.55 us  [per_device(): lax.ppermute(before[:, :half], 'y', ring('y', 1))]
    another operation x1, local copies, waits for them, and re-layouts: 0.03 us -> 1.02 us  [per_device(): held = jnp.stack(held)]
    ppermute x5, waiting for transfers between devices: 1.43 us -> 2.23 us  [per_device(): others = tuple((lax.ppermute(q, 'core', ring('core', 1)) for q in queries))]
  transfers between devices with their start and end apart: 12 -> 12, of which waited for: 8 -> 9; matrix products, arithmetic and copies ran while one was open for 6% -> 7% of each run, Pallas kernels for 11% -> 10%
where the time goes in v4:
time: 75.7 us; the launch traced here: 75.2 us
  starting transfers between devices  19.4 us (26%)
  waiting for transfers between devices  18.8 us (25%)
  blocking collectives  17.7 us (23%)
  Pallas kernels  10.1 us (13%)
  local copies, waits for them, and re-layouts  7.46 us (10%)
  other arithmetic  1.1 us (1%)
  between operations  0.83 us (1%)
    all_to_all x1, blocking collectives, per_device(): lax.all_to_all(partial.reshape(4 * TENSOR, EX_DEV, 256), S_AXES + ('tenso...  17.7 us
    pallas_call x1, Pallas kernels, project(): pl.pallas_call(project_kernel, in_specs=[pl.BlockSpec(memory_space=pl.ANY...  7.83 us
    all_to_all x1, starting transfers between devices, per_device(): lax.all_to_all(jnp.broadcast_to(sent, (4,) + sketch.shape), S_AXES, 0, 0,...  7.56 us
    unnamed x33, local copies, waits for them, and re-layouts  5.7 us
    all_to_all x1, starting transfers between devices, per_device(): got = lax.all_to_all(send, 'tensor', 0, 0, tiled=True)  5.65 us
    all_to_all x1, waiting for transfers between devices, per_device(): got = lax.all_to_all(send, 'tensor', 0, 0, tiled=True)  4.67 us
    all_to_all x1, waiting for transfers between devices, per_device(): lax.all_to_all(jnp.broadcast_to(sent, (4,) + sketch.shape), S_AXES, 0, 0,...  4.31 us
    ppermute x1, waiting for transfers between devices, per_device(): lax.ppermute(before[:, :half], 'y', ring('y', 1))  3.55 us
  transfers between devices with their start and end apart: 12, of which 9 were waited for; matrix products, arithmetic and copies ran while one was open for 7% of the time, Pallas kernels for 10%

profile of v4, /device:TPU:24, one launch (start us, length us, event | category | flops | bytes accessed | tf_op | source)
XLA Modules:
  0.0 75.2 jit_solution(14899544093043563609)
XLA Ops:
  0.6 2.0 %collective-permute-start = (bf16[128,1536]{1,0:T(8,128)(2,1)}, bf16[128,1536]{1,0:T(8,128)(2,1)S(1)}, u32[]{:S(2)}, u32[]{:S(2)}) collective-permute-start(bf16[128,1536]{1,0:T(8,128)(2,1)} %param.25), channel_id=1, source_target_pairs={{0,64},{64,128},{128,192},{192,0},{1,65},{65,129},{129,193},{193,1... | collective-permute-start | bytes 1179656 | tf_op jit(solution)/shard_map/ppermute | solution.py:167
  2.7 0.1 collective-permute-start.1
  2.7 7.8 %shard_map.140 = bf16[8,96,512]{2,1,0:T(8,128)(2,1)} custom-call(bf16[64,3584]{1,0:T(8,128)(2,1)} %bitcast.30, bf16[512,3584]{1,0:T(8,128)(2,1)} %refs_1_.1, bf16[64,3584]{1,0:T(8,128)(2,1)} %bitcast.31, bf16[512,3584]{1,0:T(8,128)(2,1)} %refs_3_.1, bf16[64,3584]{1,0:T(8,128)(2,1)} %bitcast.32, bf16[512,3584]{1,0:T(8,128)(2,1)} %refs_5_.1, ...), custom_call_target="tpu_custom_call" | custom-call | flops 1000000000 | bytes 15728640 | tf_op jit(solution)/shard_map/pallas_call | solution.py:64
  10.6 0.0 copy-start.3
  10.6 1.2 %collective-permute-done = bf16[128,1536]{1,0:T(8,128)(2,1)S(1)} collective-permute-done((bf16[128,1536]{1,0:T(8,128)(2,1)}, bf16[128,1536]{1,0:T(8,128)(2,1)S(1)}, u32[]{:S(2)}, u32[]{:S(2)}) %collective-permute-start) | collective-permute-done | bytes 393248 | tf_op jit(solution)/shard_map/ppermute | solution.py:167
  11.8 1.3 %collective-permute-done.1 = bf16[128,1536]{1,0:T(8,128)(2,1)S(1)} collective-permute-done((bf16[128,1536]{1,0:T(8,128)(2,1)}, bf16[128,1536]{1,0:T(8,128)(2,1)S(1)}, u32[]{:S(2)}, u32[]{:S(2)}) %collective-permute-start.1) | collective-permute-done | bytes 393248 | tf_op jit(solution)/shard_map/ppermute | solution.py:167
  13.1 5.7 %all-to-all-start = ((bf16[8,96,512]{2,1,0:T(8,128)(2,1)}), bf16[8,96,512]{2,1,0:T(8,128)(2,1)S(1)}, u32[]{:S(2)}, u32[]{:S(2)}) async-start(bf16[8,96,512]{2,1,0:T(8,128)(2,1)} %shard_map.140), calls=%async_computation | async-start | bytes 1572864 | tf_op jit(solution)/shard_map/all_to_all | solution.py:180
  18.8 0.3 collective-permute-start.2
  19.1 1.9 %collective-permute-start.3 = (bf16[128,768]{1,0:T(8,128)(2,1)S(1)}, bf16[128,768]{1,0:T(8,128)(2,1)S(1)}, u32[]{:S(2)}, u32[]{:S(2)}) collective-permute-start(bf16[128,768]{1,0:T(8,128)(2,1)S(1)} %slice.13), channel_id=1, source_target_pairs={{0,192},{64,0},{128,64},{192,128},{1,193},{65,1},{129,65},{193,129... | collective-permute-start | bytes 589832 | tf_op jit(solution)/shard_map/ppermute | solution.py:176
  21.0 3.5 %collective-permute-done.2 = bf16[128,768]{1,0:T(8,128)(2,1)S(1)} collective-permute-done((bf16[128,768]{1,0:T(8,128)(2,1)S(1)}, bf16[128,768]{1,0:T(8,128)(2,1)S(1)}, u32[]{:S(2)}, u32[]{:S(2)}) %collective-permute-start.2) | collective-permute-done | bytes 196640 | tf_op jit(solution)/shard_map/ppermute | solution.py:175
  24.5 1.5 %collective-permute-done.3 = bf16[128,768]{1,0:T(8,128)(2,1)S(1)} collective-permute-done((bf16[128,768]{1,0:T(8,128)(2,1)S(1)}, bf16[128,768]{1,0:T(8,128)(2,1)S(1)}, u32[]{:S(2)}, u32[]{:S(2)}) %collective-permute-start.3) | collective-permute-done | bytes 196640 | tf_op jit(solution)/shard_map/ppermute | solution.py:176
  26.0 4.7 %all-to-all-done.got = bf16[8,96,512]{2,1,0:T(8,128)(2,1)S(1)} async-done(((bf16[8,96,512]{2,1,0:T(8,128)(2,1)}), bf16[8,96,512]{2,1,0:T(8,128)(2,1)S(1)}, u32[]{:S(2)}, u32[]{:S(2)}) %all-to-all-start) | async-done | bytes 786464 | tf_op jit(solution)/shard_map/all_to_all | solution.py:180
  30.7 0.0 copy-done
  30.7 0.4 shard_map.141
  31.1 0.7 collective-permute-start.4
  31.8 0.0 copy-done.3
  31.8 0.1 collective-permute-start.5
  31.9 0.5 collective-permute-start.6
  32.4 0.1 collective-permute-start.9
  32.5 0.4 collective-permute-start.7
  32.9 0.0 collective-permute-done.4
  32.9 0.1 collective-permute-start.8
  33.1 0.0 copy-start.13
  33.1 0.5 collective-permute-done.5
  33.6 1.4 %collective-permute-done.7 = bf16[128,768]{1,0:T(8,128)(2,1)S(1)} collective-permute-done((bf16[128,768]{1,0:T(8,128)(2,1)S(1)}, bf16[128,768]{1,0:T(8,128)(2,1)S(1)}, u32[]{:S(2)}, u32[]{:S(2)}) %collective-permute-start.7) | collective-permute-done | bytes 196640 | tf_op jit(solution)/shard_map/ppermute | solution.py:179
  35.0 0.3 collective-permute-done.8
  35.3 0.0 collective-permute-done.6
  35.3 0.0 copy-done.1
  35.3 0.0 copy-done.2
  35.3 0.0 copy-done.7
  35.4 0.3 copy-done.9
  35.7 0.3 copy-done.11
  36.0 0.8 %copy-done.5 = bf16[128,1536]{1,0:T(8,128)(2,1)} copy-done((bf16[128,1536]{1,0:T(8,128)(2,1)}, bf16[128,1536]{1,0:T(8,128)(2,1)S(1)}, u32[]{:S(2)}) %copy-start.5) | copy-done | bytes 393240
  36.8 0.0 collective-permute-done.9
  36.8 1.1 %bitcast_dynamic-update-slice_fusion.5 = bf16[8,128,1536]{2,1,0:T(8,128)(2,1)S(1)} fusion(bf16[128,1536]{1,0:T(8,128)(2,1)} %param.25), kind=kLoop, calls=%fused_computation.9 | loop fusion | bytes 786432
  37.9 0.7 broadcast_in_dim.7
  38.6 7.6 %all-to-all-start.1 = ((bf16[4,16,1536]{2,1,0:T(8,128)(2,1)}), bf16[4,16,1536]{2,1,0:T(8,128)(2,1)S(1)}, u32[]{:S(2)}, u32[]{:S(2)}) async-start(bf16[4,16,1536]{2,1,0:T(8,128)(2,1)} %broadcast_in_dim.7), calls=%async_computation.1 | async-start | bytes 393216 | tf_op jit(solution)/shard_map/all_to_all | solution.py:190
  46.1 1.1 %bitcast_dynamic-update-slice_fusion.4 = bf16[8,128,1536]{2,1,0:T(8,128)(2,1)S(1)} fusion(bf16[8,128,1536]{2,1,0:T(8,128)(2,1)S(1)} %bitcast_dynamic-update-slice_fusion.5, bf16[128,1536]{1,0:T(8,128)(2,1)} %copy-done.2), kind=kLoop, calls=%fused_computation.8 | loop fusion | bytes 786432
  47.2 1.1 %fusion = bf16[8,128,1536]{2,1,0:T(8,128)(2,1)S(1)} fusion(bf16[8,128,1536]{2,1,0:T(8,128)(2,1)S(1)} %bitcast_dynamic-update-slice_fusion.4, bf16[128,768]{1,0:T(8,128)(2,1)} %copy-done.8, bf16[128,768]{1,0:T(8,128)(2,1)} %copy-done.7), kind=kLoop, calls=%fused_computation.1 | loop fusion | flops 786432 | bytes 786432
  48.3 1.0 %bitcast_dynamic-update-slice_fusion.3 = bf16[8,128,1536]{2,1,0:T(8,128)(2,1)S(1)} fusion(bf16[8,128,1536]{2,1,0:T(8,128)(2,1)S(1)} %fusion, bf16[128,1536]{1,0:T(8,128)(2,1)} %copy-done.1), kind=kLoop, calls=%fused_computation.7 | loop fusion | bytes 786432
  49.3 1.0 %bitcast_dynamic-update-slice_fusion.2 = bf16[8,128,1536]{2,1,0:T(8,128)(2,1)S(1)} fusion(bf16[8,128,1536]{2,1,0:T(8,128)(2,1)S(1)} %bitcast_dynamic-update-slice_fusion.3, bf16[128,1536]{1,0:T(8,128)(2,1)} %copy-done.4), kind=kLoop, calls=%fused_computation.6 | loop fusion | bytes 786432
  50.4 0.0 copy-done.10
  50.4 0.0 copy-done.12
  50.4 1.0 %bitcast_dynamic-update-slice_fusion.queries = bf16[8,128,1536]{2,1,0:T(8,128)(2,1)S(1)} fusion(bf16[8,128,1536]{2,1,0:T(8,128)(2,1)S(1)} %fusion.1, bf16[128,1536]{1,0:T(8,128)(2,1)} %collective-permute-done.9), kind=kLoop, calls=%fused_computation.4 | loop fusion | bytes 786432 | tf_op jit(solution)/shard_map/stack | solution.py:194
  51.5 4.3 %all-to-all-done.1.sketches = bf16[4,16,1536]{2,1,0:T(8,128)(2,1)S(1)} async-done(((bf16[4,16,1536]{2,1,0:T(8,128)(2,1)}), bf16[4,16,1536]{2,1,0:T(8,128)(2,1)S(1)}, u32[]{:S(2)}, u32[]{:S(2)}) %all-to-all-start.1) | async-done | bytes 196640 | tf_op jit(solution)/shard_map/all_to_all | solution.py:190
  55.8 1.2 %shard_map.142 = bf16[4,8,16,256]{3,2,1,0:T(8,128)(2,1)S(1)} custom-call(bf16[4,16,1536]{2,1,0:T(8,128)(2,1)S(1)} %all-to-all-done.1.sketches, bf16[8,128,1536]{2,1,0:T(8,128)(2,1)S(1)} %bitcast_dynamic-update-slice_fusion.queries), custom_call_target="tpu_custom_call" | custom-call | tf_op jit(solution)/shard_map/pallas_call | solution.py:195
  56.9 17.7 %all_to_all.15 = bf16[32,16,256]{2,1,0:T(8,128)(2,1)S(1)} all-to-all(bf16[32,16,256]{2,1,0:T(8,128)(2,1)S(1)} %bitcast.28), channel_id=1, replica_groups=mesh['y'=4,'zhh'=2,'zhl'=2,'core'=2,'tensor'=8] {'zhh','zhl','tensor'}, dimensions={0} | all-to-all | bytes 524288 | tf_op jit(solution)/shard_map/all_to_all | solution.py:200
  74.6 0.6 shard_map.143
  (24 shorter events, 0.1 us)
Async XLA Ops:
  0.6 11.1 %collective-permute-start = (bf16[128,1536]{1,0:T(8,128)(2,1)}, bf16[128,1536]{1,0:T(8,128)(2,1)S(1)}, u32[]{:S(2)}, u32[]{:S(2)}) collective-permute-start(bf16[128,1536]{1,0:T(8,128)(2,1)} %param.25), channel_id=1, source_target_pairs={{0,64},{64,128},{128,192},{192,0},{1,65},{65,129},{129,193},{193,1... | collective-permute-start | bytes 1179656 | tf_op jit(solution)/shard_map/ppermute | solution.py:167
  2.7 10.4 %collective-permute-start.1 = (bf16[128,1536]{1,0:T(8,128)(2,1)}, bf16[128,1536]{1,0:T(8,128)(2,1)S(1)}, u32[]{:S(2)}, u32[]{:S(2)}) collective-permute-start(bf16[128,1536]{1,0:T(8,128)(2,1)} %param.25), channel_id=1, source_target_pairs={{0,192},{64,0},{128,64},{192,128},{1,193},{65,1},{129,65},{193,129... | collective-permute-start | bytes 1179656 | tf_op jit(solution)/shard_map/ppermute | solution.py:167
  2.7 28.0 %copy-start = (s32[1,512]{1,0:T(1,128)S(1)}, s32[1,512]{1,0:T(1,128)}, u32[]{:S(2)}) copy-start(s32[1,512]{1,0:T(1,128)} %ids.1) | copy-start | bytes 6148
  10.6 21.2 %copy-start.3 = (bf16[128,1536]{1,0:T(8,128)(2,1)S(1)}, bf16[128,1536]{1,0:T(8,128)(2,1)}, u32[]{:S(2)}) copy-start(bf16[128,1536]{1,0:T(8,128)(2,1)} %param.25) | copy-start | bytes 1179652
  11.8 23.5 %copy-start.1 = (bf16[128,1536]{1,0:T(8,128)(2,1)}, bf16[128,1536]{1,0:T(8,128)(2,1)S(1)}, u32[]{:S(2)}) copy-start(bf16[128,1536]{1,0:T(8,128)(2,1)S(1)} %collective-permute-done) | copy-start | bytes 1179652
  13.1 22.2 %copy-start.2 = (bf16[128,1536]{1,0:T(8,128)(2,1)}, bf16[128,1536]{1,0:T(8,128)(2,1)S(1)}, u32[]{:S(2)}) copy-start(bf16[128,1536]{1,0:T(8,128)(2,1)S(1)} %collective-permute-done.1) | copy-start | bytes 1179652
  13.1 17.6 %all-to-all-start = ((bf16[8,96,512]{2,1,0:T(8,128)(2,1)}), bf16[8,96,512]{2,1,0:T(8,128)(2,1)S(1)}, u32[]{:S(2)}, u32[]{:S(2)}) async-start(bf16[8,96,512]{2,1,0:T(8,128)(2,1)} %shard_map.140), calls=%async_computation | async-start | bytes 1572864 | tf_op jit(solution)/shard_map/all_to_all | solution.py:180
  18.8 5.7 %collective-permute-start.2 = (bf16[128,768]{1,0:T(8,128)(2,1)S(1)}, bf16[128,768]{1,0:T(8,128)(2,1)S(1)}, u32[]{:S(2)}, u32[]{:S(2)}) collective-permute-start(bf16[128,768]{1,0:T(8,128)(2,1)S(1)} %slice.12), channel_id=1, source_target_pairs={{0,64},{64,128},{128,192},{192,0},{1,65},{65,129},{129,193},{193,1... | collective-permute-start | bytes 589832 | tf_op jit(solution)/shard_map/ppermute | solution.py:175
  19.1 7.0 %collective-permute-start.3 = (bf16[128,768]{1,0:T(8,128)(2,1)S(1)}, bf16[128,768]{1,0:T(8,128)(2,1)S(1)}, u32[]{:S(2)}, u32[]{:S(2)}) collective-permute-start(bf16[128,768]{1,0:T(8,128)(2,1)S(1)} %slice.13), channel_id=1, source_target_pairs={{0,192},{64,0},{128,64},{192,128},{1,193},{65,1},{129,65},{193,129... | collective-permute-start | bytes 589832 | tf_op jit(solution)/shard_map/ppermute | solution.py:176
  24.5 10.8 %copy-start.7 = (bf16[128,768]{1,0:T(8,128)(2,1)}, bf16[128,768]{1,0:T(8,128)(2,1)S(1)}, u32[]{:S(2)}) copy-start(bf16[128,768]{1,0:T(8,128)(2,1)S(1)} %collective-permute-done.2) | copy-start | bytes 589828
  26.0 9.3 %copy-start.8 = (bf16[128,768]{1,0:T(8,128)(2,1)}, bf16[128,768]{1,0:T(8,128)(2,1)S(1)}, u32[]{:S(2)}) copy-start(bf16[128,768]{1,0:T(8,128)(2,1)S(1)} %collective-permute-done.3) | copy-start | bytes 589828
  31.1 1.8 %collective-permute-start.4 = (bf16[16,512]{1,0:T(8,128)(2,1)S(1)}, bf16[16,512]{1,0:T(8,128)(2,1)S(1)}, u32[]{:S(2)}, u32[]{:S(2)}) collective-permute-start(bf16[16,512]{1,0:T(8,128)(2,1)S(1)} %slice.17), channel_id=1, source_target_pairs={{3,2},{4,5},{11,10},{12,13},{19,18},{20,21},{27,26},{28,29},{35,34... | collective-permute-start | bytes 49160 | tf_op jit(solution)/shard_map/ppermute | solution.py:184
  31.8 1.8 %collective-permute-start.5 = (bf16[128,1536]{1,0:T(8,128)(2,1)S(1)}, bf16[128,1536]{1,0:T(8,128)(2,1)S(1)}, u32[]{:S(2)}, u32[]{:S(2)}) collective-permute-start(bf16[128,1536]{1,0:T(8,128)(2,1)S(1)} %copy-done.3), channel_id=1, source_target_pairs={{0,8},{8,0},{1,9},{9,1},{2,10},{10,2},{3,11},{11,3},{4,12},{12,4},... | collective-permute-start | bytes 1179656 | tf_op jit(solution)/shard_map/ppermute | solution.py:179
  31.9 3.4 %collective-permute-start.6 = (bf16[128,1536]{1,0:T(8,128)(2,1)S(1)}, bf16[128,1536]{1,0:T(8,128)(2,1)S(1)}, u32[]{:S(2)}, u32[]{:S(2)}) collective-permute-start(bf16[128,1536]{1,0:T(8,128)(2,1)S(1)} %collective-permute-done.1), channel_id=1, source_target_pairs={{0,8},{8,0},{1,9},{9,1},{2,10},{10,2},{3,11},{11,3},{4,12},{12,4},... | collective-permute-start | bytes 1179656 | tf_op jit(solution)/shard_map/ppermute | solution.py:179
  32.4 4.4 %collective-permute-start.9 = (bf16[128,1536]{1,0:T(8,128)(2,1)S(1)}, bf16[128,1536]{1,0:T(8,128)(2,1)}, u32[]{:S(2)}, u32[]{:S(2)}) collective-permute-start(bf16[128,1536]{1,0:T(8,128)(2,1)S(1)} %collective-permute-done), channel_id=1, source_target_pairs={{0,8},{8,0},{1,9},{9,1},{2,10},{10,2},{3,11},{11,3},{4,12},{12,4},... | collective-permute-start | bytes 1179656 | tf_op jit(solution)/shard_map/ppermute | solution.py:179
  32.5 2.5 %collective-permute-start.7 = (bf16[128,768]{1,0:T(8,128)(2,1)S(1)}, bf16[128,768]{1,0:T(8,128)(2,1)S(1)}, u32[]{:S(2)}, u32[]{:S(2)}) collective-permute-start(bf16[128,768]{1,0:T(8,128)(2,1)S(1)} %collective-permute-done.2), channel_id=1, source_target_pairs={{0,8},{8,0},{1,9},{9,1},{2,10},{10,2},{3,11},{11,3},{4,12},{12,4},... | collective-permute-start | bytes 589832 | tf_op jit(solution)/shard_map/ppermute | solution.py:179
  32.9 2.4 %collective-permute-start.8 = (bf16[128,768]{1,0:T(8,128)(2,1)S(1)}, bf16[128,768]{1,0:T(8,128)(2,1)S(1)}, u32[]{:S(2)}, u32[]{:S(2)}) collective-permute-start(bf16[128,768]{1,0:T(8,128)(2,1)S(1)} %collective-permute-done.3), channel_id=1, source_target_pairs={{0,8},{8,0},{1,9},{9,1},{2,10},{10,2},{3,11},{11,3},{4,12},{12,4},... | collective-permute-start | bytes 589832 | tf_op jit(solution)/shard_map/ppermute | solution.py:179
  33.1 4.8 %copy-start.13 = (bf16[16,1536]{1,0:T(8,128)(2,1)}, bf16[16,1536]{1,0:T(8,128)(2,1)S(1)}, u32[]{:S(2)}) copy-start(bf16[16,1536]{1,0:T(8,128)(2,1)S(1)} %slice_add_fusion) | copy-start | bytes 147460
  33.6 1.7 %copy-start.4 = (bf16[128,1536]{1,0:T(8,128)(2,1)}, bf16[128,1536]{1,0:T(8,128)(2,1)S(1)}, u32[]{:S(2)}) copy-start(bf16[128,1536]{1,0:T(8,128)(2,1)S(1)} %collective-permute-done.5) | copy-start | bytes 1179652
  35.0 0.7 copy-start.9
  35.3 0.7 copy-start.11
  36.0 0.8 %copy-start.5 = (bf16[128,1536]{1,0:T(8,128)(2,1)}, bf16[128,1536]{1,0:T(8,128)(2,1)S(1)}, u32[]{:S(2)}) copy-start(bf16[128,1536]{1,0:T(8,128)(2,1)S(1)} %collective-permute-done.6) | copy-start | bytes 1179652
  36.8 13.6 %copy-start.10 = (bf16[128,768]{1,0:T(8,128)(2,1)S(1)}, bf16[128,768]{1,0:T(8,128)(2,1)}, u32[]{:S(2)}) copy-start(bf16[128,768]{1,0:T(8,128)(2,1)} %copy-done.9) | copy-start | bytes 589828
  38.6 17.2 %all-to-all-start.1 = ((bf16[4,16,1536]{2,1,0:T(8,128)(2,1)}), bf16[4,16,1536]{2,1,0:T(8,128)(2,1)S(1)}, u32[]{:S(2)}, u32[]{:S(2)}) async-start(bf16[4,16,1536]{2,1,0:T(8,128)(2,1)} %broadcast_in_dim.7), calls=%async_computation.1 | async-start | bytes 393216 | tf_op jit(solution)/shard_map/all_to_all | solution.py:190
  46.1 4.2 %copy-start.6 = (bf16[128,1536]{1,0:T(8,128)(2,1)S(1)}, bf16[128,1536]{1,0:T(8,128)(2,1)}, u32[]{:S(2)}) copy-start(bf16[128,1536]{1,0:T(8,128)(2,1)} %copy-done.5) | copy-start | bytes 1179652
  46.1 4.3 %copy-start.12 = (bf16[128,768]{1,0:T(8,128)(2,1)S(1)}, bf16[128,768]{1,0:T(8,128)(2,1)}, u32[]{:S(2)}) copy-start(bf16[128,768]{1,0:T(8,128)(2,1)} %copy-done.11) | copy-start | bytes 589828
